TPU v7x, 32 devices: a whole 2x2x4 slice. The times are simulated.
32 devices in a mesh: fsdp: 32 (over z, y, x, core).
Axes of the slice: x: 2, y: 2, z: 4, core: 2. Of those that a mesh axis runs over, the one named last changes fastest.
Arguments:
- tokens: bfloat16 [128, 196, 768], P('fsdp'), may hold values from -6 to 6
- cotangent: bfloat16 [128, 196, 768], P('fsdp'), may hold values from -6 to 6
- lengths: int32 [128], P('fsdp'), may hold values from 144 to 196, as said below
- ln1_gain: bfloat16 [768], P('fsdp'), may hold values from 0.5 to 1.5
- ln1_bias: bfloat16 [768], P('fsdp'), may hold values from -3 to 3
- qkv_weight: bfloat16 [768, 2304], P(None, 'fsdp'), may hold values from -0.21875 to 0.21875
- q_bias: bfloat16 [768], P('fsdp'), may hold values from -3 to 3
- v_bias: bfloat16 [768], P('fsdp'), may hold values from -3 to 3
- out_weight: bfloat16 [768, 768], P(None, 'fsdp'), may hold values from -0.625 to 0.625
- out_bias: bfloat16 [768], P('fsdp'), may hold values from -3 to 3
- ln2_gain: bfloat16 [768], P('fsdp'), may hold values from 0.5 to 1.5
- ln2_bias: bfloat16 [768], P('fsdp'), may hold values from -3 to 3
- up_weight: bfloat16 [768, 3072], P(None, 'fsdp'), may hold values from -0.21875 to 0.21875
- up_bias: bfloat16 [3072], P('fsdp'), may hold values from -3 to 3
- down_weight: bfloat16 [3072, 768], P(None, 'fsdp'), may hold values from -0.109375 to 0.109375
- down_bias: bfloat16 [768], P('fsdp'), may hold values from -3 to 3
Outputs:
- output: bfloat16 [128, 196, 768], P('fsdp')
- input_grad: float32 [128, 196, 768], P('fsdp')
- ln1_gain_grad: float32 [768], P('fsdp')
- ln1_bias_grad: float32 [768], P('fsdp')
- qkv_weight_grad: float32 [768, 2304], P(None, 'fsdp')
- q_bias_grad: float32 [768], P('fsdp')
- v_bias_grad: float32 [768], P('fsdp')
- out_weight_grad: float32 [768, 768], P(None, 'fsdp')
- out_bias_grad: float32 [768], P('fsdp')
- ln2_gain_grad: float32 [768], P('fsdp')
- ln2_bias_grad: float32 [768], P('fsdp')
- up_weight_grad: float32 [768, 3072], P(None, 'fsdp')
- up_bias_grad: float32 [3072], P('fsdp')
- down_weight_grad: float32 [3072, 768], P(None, 'fsdp')
- down_bias_grad: float32 [768], P('fsdp')
Inputs may be any that keep to these rules, and one draw needn't show every extreme that they name: `lengths`: each image has 144 or 196 patches; some image has 196.
All inputs are finite; a program needn't handle non-finite values.
Results may differ from a plain program's by a relative error of at most 0.012.
Values may be sent and summed in bfloat16 or wider, within the bound.
No kernel may reach another device: no remote copies, remote signals or barrier semaphores. Data moves between devices by JAX's collectives and lax.ppermute only.
A program may use at most 192 MiB of HBM per device.

v0:
```python
import jax
import jax.numpy as jnp
from jax import lax
from jax.sharding import PartitionSpec as P

H = 12
HD = 64


epsilon = 1e-06


def norm_parts(values):
    center = values - jnp.mean(values, axis=-1, keepdims=True)
    rscale = lax.rsqrt(jnp.mean(center * center, axis=-1, keepdims=True) + epsilon)
    return (center * rscale, rscale)


def norm_back(grad_normal, normal, rscale):
    grad_mean = jnp.mean(grad_normal, axis=-1, keepdims=True)
    grad_cross = jnp.mean(grad_normal * normal, axis=-1, keepdims=True)
    return rscale * (grad_normal - grad_mean - normal * grad_cross)


def exact_gelu(values):
    return jax.nn.gelu(values, approximate=False)


def attention_forward(tokens, lengths, attn_params):
    ln_gain, ln_bias, qkv_weight, q_bias, v_bias, out_weight, out_bias = attn_params
    image_count, slot_count, model_width = tokens.shape
    inputs = tokens.astype(jnp.float32)
    normal, rscale = norm_parts(inputs)
    normed_low = (normal * ln_gain.astype(jnp.float32) + ln_bias.astype(jnp.float32)).astype(
        jnp.bfloat16
    )
    qkv_bias = jnp.concatenate([q_bias, jnp.zeros_like(q_bias), v_bias]).astype(jnp.float32)
    qkv_rows = (
        jnp.einsum("gsd,de->gse", normed_low, qkv_weight, preferred_element_type=jnp.float32)
        + qkv_bias
    )
    qkv_rows = qkv_rows.astype(jnp.bfloat16).reshape(image_count, slot_count, 3, H, HD)
    query_rows = qkv_rows[:, :, 0]
    key_rows = qkv_rows[:, :, 1]
    value_rows = qkv_rows[:, :, 2]
    key_live = lax.broadcasted_iota(jnp.int32, (image_count, slot_count), 1) < lengths[:, None]
    scores = jnp.einsum(
        "gqhe,gkhe->ghqk", query_rows, key_rows, preferred_element_type=jnp.float32
    ) * HD ** (-0.5)
    scores = jnp.where(key_live[:, None, None, :], scores, -1e30)
    attend = jax.nn.softmax(scores, axis=-1)
    attend_low = attend.astype(jnp.bfloat16)
    mixture = jnp.einsum(
        "ghqk,gkhe->gqhe", attend_low, value_rows, preferred_element_type=jnp.float32
    )
    mixture_low = mixture.reshape(image_count, slot_count, model_width).astype(jnp.bfloat16)
    branch = jnp.einsum(
        "gsd,de->gse", mixture_low, out_weight, preferred_element_type=jnp.float32
    ) + out_bias.astype(jnp.float32)
    middle = inputs + branch
    saved = (
        inputs,
        normal,
        rscale,
        normed_low,
        query_rows,
        key_rows,
        value_rows,
        attend,
        attend_low,
        mixture_low,
    )
    return (middle, saved)


def attention_backward(grad_middle, saved, attn_params):
    ln_gain, ln_bias, qkv_weight, q_bias, v_bias, out_weight, out_bias = attn_params
    (
        inputs,
        normal,
        rscale,
        normed_low,
        query_rows,
        key_rows,
        value_rows,
        attend,
        attend_low,
        mixture_low,
    ) = saved
    image_count, slot_count, model_width = inputs.shape
    scale_factor = HD ** (-0.5)
    grad_branch = grad_middle.astype(jnp.bfloat16)
    out_bias_grad = jnp.sum(grad_branch.astype(jnp.float32), axis=(0, 1))
    grad_mixture = jnp.einsum(
        "gse,de->gsd", grad_branch, out_weight, preferred_element_type=jnp.float32
    )
    grad_mixture = grad_mixture.astype(jnp.bfloat16).reshape(image_count, slot_count, H, HD)
    grad_attend = jnp.einsum(
        "gqhe,gkhe->ghqk", grad_mixture, value_rows, preferred_element_type=jnp.float32
    )
    grad_value = jnp.einsum(
        "ghqk,gqhe->gkhe", attend_low, grad_mixture, preferred_element_type=jnp.float32
    )
    row_inner = jnp.sum(grad_attend * attend, axis=-1, keepdims=True)
    grad_scores = (attend * (grad_attend - row_inner)).astype(jnp.bfloat16)
    grad_query = (
        jnp.einsum("ghqk,gkhe->gqhe", grad_scores, key_rows, preferred_element_type=jnp.float32)
        * scale_factor
    )
    grad_key = (
        jnp.einsum("ghqk,gqhe->gkhe", grad_scores, query_rows, preferred_element_type=jnp.float32)
        * scale_factor
    )
    grad_qkv = jnp.stack([grad_query, grad_key, grad_value], axis=2).astype(jnp.bfloat16)
    grad_qkv = grad_qkv.reshape(image_count, slot_count, 3 * model_width)
    qkv_bias_sum = jnp.sum(grad_qkv.astype(jnp.float32), axis=(0, 1))
    grad_normed = jnp.einsum(
        "gse,de->gsd", grad_qkv, qkv_weight, preferred_element_type=jnp.float32
    )
    ln_gain_grad = jnp.sum(grad_normed * normal, axis=(0, 1))
    ln_bias_grad = jnp.sum(grad_normed, axis=(0, 1))
    grad_inputs = grad_middle + norm_back(grad_normed * ln_gain.astype(jnp.float32), normal, rscale)
    vectors = (
        ln_gain_grad,
        ln_bias_grad,
        qkv_bias_sum[:model_width],
        qkv_bias_sum[2 * model_width :],
        out_bias_grad,
    )
    operands = (normed_low, grad_qkv, mixture_low, grad_branch)
    return (grad_inputs, vectors, operands)


def feed_forward(middle, feed_params):
    ln_gain, ln_bias, up_weight, up_bias, down_weight, down_bias = feed_params
    normal, rscale = norm_parts(middle)
    normed_low = (normal * ln_gain.astype(jnp.float32) + ln_bias.astype(jnp.float32)).astype(
        jnp.bfloat16
    )
    pre_gelu = jnp.einsum(
        "gsd,df->gsf", normed_low, up_weight, preferred_element_type=jnp.float32
    ) + up_bias.astype(jnp.float32)
    hidden, gelu_pullback = jax.vjp(exact_gelu, pre_gelu)
    hidden_low = hidden.astype(jnp.bfloat16)
    feed = jnp.einsum(
        "gsf,fd->gsd", hidden_low, down_weight, preferred_element_type=jnp.float32
    ) + down_bias.astype(jnp.float32)
    saved = (normal, rscale, normed_low, gelu_pullback, hidden_low)
    return (middle + feed, saved)


def feed_backward(grad_output, saved, feed_params):
    ln_gain, ln_bias, up_weight, up_bias, down_weight, down_bias = feed_params
    normal, rscale, normed_low, gelu_pullback, hidden_low = saved
    grad_feed = grad_output.astype(jnp.bfloat16)
    down_bias_grad = jnp.sum(grad_feed.astype(jnp.float32), axis=(0, 1))
    grad_hidden = jnp.einsum(
        "gsd,fd->gsf", grad_feed, down_weight, preferred_element_type=jnp.float32
    )
    grad_pre = gelu_pullback(grad_hidden)[0].astype(jnp.bfloat16)
    up_bias_grad = jnp.sum(grad_pre.astype(jnp.float32), axis=(0, 1))
    grad_normed = jnp.einsum("gsf,df->gsd", grad_pre, up_weight, preferred_element_type=jnp.float32)
    ln_gain_grad = jnp.sum(grad_normed * normal, axis=(0, 1))
    ln_bias_grad = jnp.sum(grad_normed, axis=(0, 1))
    grad_middle = grad_output + norm_back(grad_normed * ln_gain.astype(jnp.float32), normal, rscale)
    vectors = (ln_gain_grad, ln_bias_grad, up_bias_grad, down_bias_grad)
    operands = (normed_low, grad_pre, hidden_low, grad_feed)
    return (grad_middle, vectors, operands)


def cross_rows(left, right):
    return jnp.einsum("gsd,gse->de", left, right, preferred_element_type=jnp.float32)


def shards(
    tokens,
    cotangent,
    lengths,
    ln1_gain,
    ln1_bias,
    qkv_weight,
    q_bias,
    v_bias,
    out_weight,
    out_bias,
    ln2_gain,
    ln2_bias,
    up_weight,
    up_bias,
    down_weight,
    down_bias,
):
    attn_full = (
        lax.all_gather(ln1_gain, "fsdp", axis=0, tiled=True),
        lax.all_gather(ln1_bias, "fsdp", axis=0, tiled=True),
        lax.all_gather(qkv_weight, "fsdp", axis=1, tiled=True),
        lax.all_gather(q_bias, "fsdp", axis=0, tiled=True),
        lax.all_gather(v_bias, "fsdp", axis=0, tiled=True),
        lax.all_gather(out_weight, "fsdp", axis=1, tiled=True),
        lax.all_gather(out_bias, "fsdp", axis=0, tiled=True),
    )
    middle, unused_attn = attention_forward(tokens, lengths, attn_full)
    feed_full = (
        lax.all_gather(ln2_gain, "fsdp", axis=0, tiled=True),
        lax.all_gather(ln2_bias, "fsdp", axis=0, tiled=True),
        lax.all_gather(up_weight, "fsdp", axis=1, tiled=True),
        lax.all_gather(up_bias, "fsdp", axis=0, tiled=True),
        lax.all_gather(down_weight, "fsdp", axis=1, tiled=True),
        lax.all_gather(down_bias, "fsdp", axis=0, tiled=True),
    )
    output, unused_feed = feed_forward(middle, feed_full)
    feed_back = (
        lax.all_gather(ln2_gain, "fsdp", axis=0, tiled=True),
        lax.all_gather(ln2_bias, "fsdp", axis=0, tiled=True),
        lax.all_gather(up_weight, "fsdp", axis=1, tiled=True),
        lax.all_gather(up_bias, "fsdp", axis=0, tiled=True),
        lax.all_gather(down_weight, "fsdp", axis=1, tiled=True),
        lax.all_gather(down_bias, "fsdp", axis=0, tiled=True),
    )
    attn_back = (
        lax.all_gather(ln1_gain, "fsdp", axis=0, tiled=True),
        lax.all_gather(ln1_bias, "fsdp", axis=0, tiled=True),
        lax.all_gather(qkv_weight, "fsdp", axis=1, tiled=True),
        lax.all_gather(q_bias, "fsdp", axis=0, tiled=True),
        lax.all_gather(v_bias, "fsdp", axis=0, tiled=True),
        lax.all_gather(out_weight, "fsdp", axis=1, tiled=True),
        lax.all_gather(out_bias, "fsdp", axis=0, tiled=True),
    )
    again_output, feed_saved = feed_forward(middle, feed_back)
    grad_middle, feed_vectors, feed_operands = feed_backward(
        cotangent.astype(jnp.float32), feed_saved, feed_back
    )
    normed_two, grad_pre, hidden_low, grad_feed = feed_operands
    up_grad = cross_rows(normed_two, grad_pre)
    down_grad = cross_rows(hidden_low, grad_feed)
    feed_sums = (
        lax.psum_scatter(feed_vectors[0], "fsdp", scatter_dimension=0, tiled=True),
        lax.psum_scatter(feed_vectors[1], "fsdp", scatter_dimension=0, tiled=True),
        lax.psum_scatter(up_grad, "fsdp", scatter_dimension=1, tiled=True),
        lax.psum_scatter(feed_vectors[2], "fsdp", scatter_dimension=0, tiled=True),
        lax.psum_scatter(down_grad, "fsdp", scatter_dimension=1, tiled=True),
        lax.psum_scatter(feed_vectors[3], "fsdp", scatter_dimension=0, tiled=True),
    )
    again_middle, attn_saved = attention_forward(tokens, lengths, attn_back)
    grad_inputs, attn_vectors, attn_operands = attention_backward(
        grad_middle, attn_saved, attn_back
    )
    normed_one, grad_qkv, mixture_low, grad_branch = attn_operands
    qkv_grad = cross_rows(normed_one, grad_qkv)
    out_grad = cross_rows(mixture_low, grad_branch)
    attn_sums = (
        lax.psum_scatter(attn_vectors[0], "fsdp", scatter_dimension=0, tiled=True),
        lax.psum_scatter(attn_vectors[1], "fsdp", scatter_dimension=0, tiled=True),
        lax.psum_scatter(qkv_grad, "fsdp", scatter_dimension=1, tiled=True),
        lax.psum_scatter(attn_vectors[2], "fsdp", scatter_dimension=0, tiled=True),
        lax.psum_scatter(attn_vectors[3], "fsdp", scatter_dimension=0, tiled=True),
        lax.psum_scatter(out_grad, "fsdp", scatter_dimension=1, tiled=True),
        lax.psum_scatter(attn_vectors[4], "fsdp", scatter_dimension=0, tiled=True),
    )
    return (
        output.astype(jnp.bfloat16),
        grad_inputs,
        attn_sums[0],
        attn_sums[1],
        attn_sums[2],
        attn_sums[3],
        attn_sums[4],
        attn_sums[5],
        attn_sums[6],
        feed_sums[0],
        feed_sums[1],
        feed_sums[2],
        feed_sums[3],
        feed_sums[4],
        feed_sums[5],
    )


def solution(mesh):
    return jax.shard_map(
        shards,
        mesh=mesh,
        in_specs=(
            P("fsdp", None, None),
            P("fsdp", None, None),
            P("fsdp"),
            P("fsdp"),
            P("fsdp"),
            P(None, "fsdp"),
            P("fsdp"),
            P("fsdp"),
            P(None, "fsdp"),
            P("fsdp"),
            P("fsdp"),
            P("fsdp"),
            P(None, "fsdp"),
            P("fsdp"),
            P(None, "fsdp"),
            P("fsdp"),
        ),
        out_specs=(
            P("fsdp", None, None),
            P("fsdp", None, None),
            P("fsdp"),
            P("fsdp"),
            P(None, "fsdp"),
            P("fsdp"),
            P("fsdp"),
            P(None, "fsdp"),
            P("fsdp"),
            P("fsdp"),
            P("fsdp"),
            P(None, "fsdp"),
            P("fsdp"),
            P(None, "fsdp"),
            P("fsdp"),
        ),
        check_vma=False,
    )
```

profile of v0, /device:TPU:0, one launch (start us, length us, event | category | flops | bytes accessed | tf_op | source)
XLA Modules:
  0.0 815.0 jit_solution(197248020877360814)
XLA Ops:
  10.0 0.8 dynamic-update-slice
  11.7 0.8 dynamic-update-slice.2
  16.7 0.8 dynamic-update-slice.7
  17.6 42.9 %all-reduce.19 = (bf16[768]{0:T(1024)(128)(2,1)S(1)}, bf16[768]{0:T(1024)(128)(2,1)S(1)}, bf16[768]{0:T(1024)(128)(2,1)S(1)}, bf16[768]{0:T(1024)(128)(2,1)S(1)}...) all-reduce(bf16[768]{0:T(1024)(128)(2,1)S(1)} %dynamic-update-slice, ...), channel_id=1, replica_groups=mesh['fsdp'=32] {'fsdp'}, use_global_device_ids=true, to_apply=%add.3 | all-reduce | flops 9216 | bytes 36864
  60.4 1.5 convert_reduce_fusion.2
  62.0 1.8 fusion.34
  64.5 9.4 %all-gather.5.cloned.1.call-done = bf16[768,2304]{0,1:T(8,128)(2,1)} async-done(((bf16[768,72]{0,1:T(8,128)(2,1)}), bf16[768,2304]{0,1:T(8,128)(2,1)}) %all-gather.5.cloned.1.call-update) | async-done | bytes 3538960 | tf_op jit(solution)/shard_map/all_gather | solution.py:196
  73.9 7.5 add_convert_fusion.1
  81.4 6.3 copy.69
  87.7 3.4 fusion.50
  91.1 4.7 fusion.65
  95.8 3.8 copy-done.3
  99.6 3.8 fusion.44
  103.4 26.4 %all-gather.7.cloned.1.call-done = bf16[768,768]{0,1:T(8,128)(2,1)} async-done(((bf16[768,24]{0,1:T(8,128)(2,1)}), bf16[768,768]{0,1:T(8,128)(2,1)}) %all-gather.7.cloned.1.call-update) | async-done | bytes 1179664 | tf_op jit(solution)/shard_map/all_gather | solution.py:199
  129.8 3.3 fusion.66
  133.1 1.5 copy-done.5
  135.0 60.3 %all-gather.9.cloned.1.call-done = bf16[768,3072]{0,1:T(8,128)(2,1)} async-done(((bf16[768,96]{0,1:T(8,128)(2,1)}), bf16[768,3072]{0,1:T(8,128)(2,1)}) %all-gather.9.cloned.1.call-update) | async-done | bytes 4718608 | tf_op jit(solution)/shard_map/all_gather | solution.py:206
  195.3 9.6 %fusion.40 = (u8[196,3072]{1,0:T(8,128)(4,1)S(1)}, u8[196,3072]{1,0:T(8,128)(4,1)S(1)}, f32[4,196,3072]{2,1,0:T(8,128)S(1)}) fusion(f32[3072]{0:T(1024)S(1)} %convert_element_type.122, bf16[768,3072]{0,1:T(8,128)(2,1)} %all-gather.9.cloned.1.call-done, f32[4,196,768]{2,1,0:T(8,128)} %copy-done.5, f32[768]{0:T(1024)S(1)} %convert_element_type.120, ...), kind=kOutput, calls=%fused_computation.80 | convolution fusion | flops 3734900736 | bytes 17989760 | tf_op jit(solution)/shard_map/gsd,df->gsf/dot_general | solution.py:140
  204.9 3.7 copy-done.4
  208.6 23.7 %multiply_convert_fusion.1 = (bf16[4,196,3072]{2,1,0:T(8,128)(2,1)}, f32[4,196,3072]{2,1,0:T(8,128)}) fusion(f32[4,196,3072]{2,1,0:T(8,128)S(1)} %get-tuple-element.101, f32[3072]{0:T(1024)S(1)} %convert_element_type.122, u8[196,3072]{1,0:T(8,128)(4,1)S(1)} %get-tuple-element.61, u8[196,3072]{1,0:T(8,128)(4,1)S(1)} %get-tuple-element.60), kind=kLoop, calls=%fused_computation.12 | loop fusion | flops 170999808 | bytes 25300992 | tf_op jit(solution)/shard_map/convert_element_type | solution.py:144
  232.3 28.3 %all-gather.11.cloned.1.call-done = bf16[3072,768]{0,1:T(8,128)(2,1)} async-done(((bf16[3072,24]{0,1:T(8,128)(2,1)}), bf16[3072,768]{0,1:T(8,128)(2,1)}) %all-gather.11.cloned.1.call-update) | async-done | bytes 4718608 | tf_op jit(solution)/shard_map/all_gather | solution.py:208
  260.6 12.6 %convert_reduce_fusion = (f32[3072]{0:T(1024)S(1)}, bf16[4,196,3072]{2,1,0:T(8,128)(2,1)S(1)}) fusion(f32[4,196,3072]{2,1,0:T(8,128)} %get-tuple-element.93, bf16[3072,768]{0,1:T(8,128)(2,1)} %all-gather.11.cloned.1.call-done, bf16[4,196,768]{2,0,1:T(4,128)(2,1)S(1)} %copy-done.9, f32[4,196,3072]{2,1,0:T(8,128)} %copy-done.4, f32[3072]{0:T(1024)S(1)} %convert_element_type.122), kind=kOutput, calls=%fused_computation.8 | convolution fusion | flops 3740316672 | bytes 30031872 | tf_op jit(solution)/shard_map/gsd,fd->gsf/dot_general | solution.py:157
  273.2 8.7 %multiply_reduce_fusion.1 = (f32[768]{0:T(1024)S(1)}, f32[4,196]{1,0:T(4,128)S(1)}, f32[4,196]{1,0:T(4,128)S(1)}, f32[768]{0:T(1024)S(1)}, f32[4,196,768]{2,1,0:T(8,128)S(1)}) fusion(f32[4,196,768]{2,1,0:T(8,128)S(1)} %copy-done.6, f32[4,196]{1,0:T(4,128)S(1)} %add_rsqrt_fusion, f32[4,196]{1,0:T(4,128)S(1)} %broadcast_multiply_fusion.4, ...), kind=kOutput, calls=%fused_computation.69 | convolution fusion | flops 3704792064 | bytes 14374144 | tf_op jit(solution)/shard_map/gsf,df->gsd/dot_general | solution.py:162
  281.9 1.1 convert_reduce_fusion.4
  283.0 1.4 copy-done.2
  284.5 2.9 convolution_bitcast_fusion.3
  287.4 3.9 convolution_convert_fusion
  291.2 1.6 copy.77
  292.9 8.3 %multiply_reduce_fusion = (f32[4,12,196]{2,1,0:T(8,128)S(1)}, f32[4,12,196,196]{2,3,1,0:T(8,128)}) fusion(f32[4,12,196,196]{2,3,1,0:T(8,128)} %copy-done.3, f32[4,12,196]{2,1,0:T(8,128)S(1)} %get-tuple-element.97, bf16[4,196,12,64]{1,3,2,0:T(8,128)(2,1)S(1)} %bitcast.99, bf16[4,196,3,12,64]{1,4,3,2,0:T(8,128)(2,1)} %bitcast.92), kind=kOutput, calls=%fused_computation.10 | convolution fusion | flops 241550400 | bytes 20058624 | tf_op jit(solution)/shard_map/gqhe,gkhe->ghqk/dot_general | solution.py:98
  301.5 11.4 %multiply_convert_fusion = bf16[4,12,196,196]{2,3,1,0:T(8,128)(2,1)} fusion(f32[4,12,196,196]{2,3,1,0:T(8,128)} %get-tuple-element.104, f32[4,12,196]{2,1,0:T(8,128)S(1)} %get-tuple-element.103, f32[4,12,196,196]{2,3,1,0:T(8,128)} %copy-done.3, f32[4,12,196]{2,1,0:T(8,128)S(1)} %get-tuple-element.97), kind=kLoop, calls=%fused_computation.9 | loop fusion | flops 7375872 | bytes 18514944 | tf_op jit(solution)/shard_map/convert_element_type | solution.py:105
  312.8 4.8 multiply_bitcast_fusion
  317.6 2.5 multiply_bitcast_fusion.1
  320.1 5.6 fusion.41
  325.8 1.2 convert_reduce_fusion.1
  327.7 2.2 copy-done.8
  329.9 6.8 convolution_bitcast_fusion.2
  336.8 10.5 %convolution_bitcast_fusion.1 = f32[768,3072]{0,1:T(8,128)} fusion(bf16[4,196,3072]{2,1,0:T(8,128)(2,1)} %copy-done.14, f32[4,196,768]{2,1,0:T(8,128)} %copy-done.5, f32[768]{0:T(1024)S(1)} %convert_element_type.120, f32[768]{0:T(1024)S(1)} %convert_element_type.119, f32[4,196]{1,0:T(4,128)S(1)} %add_rsqrt_fusion, f32[4,196]{1,0:T(4,128)S(1)} %broadcast_multiply_fusion.4), kind=kOutput, calls=%fused_computation.32 | convolution fusion | flops 3702386688 | bytes 16674944 | tf_op jit(solution)/shard_map/gsd,gse->de/dot_general | solution.py:172
  347.7 1.0 copy-done.10
  348.7 9.9 %convolution_bitcast_fusion = f32[3072,768]{0,1:T(8,128)} fusion(bf16[4,196,3072]{2,1,0:T(8,128)(2,1)} %get-tuple-element.92, bf16[4,196,768]{2,0,1:T(4,128)(2,1)S(1)} %copy-done.10), kind=kOutput, calls=%fused_computation.31 | convolution fusion | flops 3699376128 | bytes 15458304 | tf_op jit(solution)/shard_map/gsd,gse->de/dot_general | solution.py:172
  359.5 8.6 %fusion.33 = (f32[768]{0:T(1024)S(1)}, f32[4,196]{1,0:T(4,128)S(1)}, f32[4,196]{1,0:T(4,128)S(1)}, f32[768]{0:T(1024)S(1)}, f32[4,196,768]{2,1,0:T(8,128)}) fusion(f32[4,196]{1,0:T(4,128)S(1)} %add_rsqrt_fusion.1, f32[4,196]{1,0:T(4,128)S(1)} %broadcast_multiply_fusion.5, bf16[4,196,768]{2,0,1:T(4,128)(2,1)S(1)} %copy-done.1, ...), kind=kOutput, calls=%fused_computation.67 | convolution fusion | flops 2780550144 | bytes 10786048 | tf_op jit(solution)/shard_map/gse,de->gsd/dot_general | solution.py:117
  368.1 40.8 %all-reduce.18 = (f32[768]{0:T(1024)S(1)}, f32[768]{0:T(1024)S(1)}, f32[768]{0:T(1024)S(1)}, f32[768]{0:T(1024)S(1)}, f32[768]{0:T(1024)S(1)}, /*index=5*/f32[76...) all-reduce(f32[768]{0:T(1024)S(1)} %get-tuple-element.64, ...), channel_id=2, replica_groups=mesh['fsdp'=32] {'fsdp'}, use_global_device_ids=true, to_apply=%region_12.13.clone | all-reduce | flops 9216 | bytes 73728
  413.6 3.2 fusion.32
  416.8 2.4 copy.87
  419.2 6.6 add_convert_fusion.2
  425.8 1.5 copy.86
  427.9 96.6 %reduce-scatter.5.cloned.1.call-done = f32[768,72]{0,1:T(8,128)} async-done(((f32[768,2304]{0,1:T(8,128)}), f32[768,72]{0,1:T(8,128)}) %reduce-scatter.5.cloned.1.call-update) | async-done | bytes 221200 | tf_op jit(solution)/shard_map/reduce_scatter | solution.py:254
  524.5 141.1 %reduce-scatter.9.cloned.1.call-done = f32[768,96]{0,1:T(8,128)} async-done(((f32[768,3072]{0,1:T(8,128)}), f32[768,96]{0,1:T(8,128)}) %reduce-scatter.9.cloned.1.call-update) | async-done | bytes 294928 | tf_op jit(solution)/shard_map/reduce_scatter | solution.py:239
  665.7 142.3 %reduce-scatter.11.cloned.1.call-done = f32[3072,24]{0,1:T(8,128)} async-done(((f32[3072,768]{0,1:T(8,128)}), f32[3072,24]{0,1:T(8,128)}) %reduce-scatter.11.cloned.1.call-update) | async-done | bytes 294928 | tf_op jit(solution)/shard_map/reduce_scatter | solution.py:241
  (92 shorter events, 16.6 us)
Async XLA Ops:
  7.2 66.7 %all-gather.5.cloned.1.call-start = ((), (), s32[]{:S(2)}) async-start(), calls=%async_computation.4 | async-start | bytes 3649536 | tf_op jit(solution)/shard_map/all_gather | solution.py:196
  7.9 121.9 %all-gather.7.cloned.1.call-start = ((), (), s32[]{:S(2)}) async-start(), calls=%async_computation.5 | async-start | bytes 1216512 | tf_op jit(solution)/shard_map/all_gather | solution.py:199
  8.7 186.7 %all-gather.9.cloned.1.call-start = ((), (), s32[]{:S(2)}) async-start(), calls=%async_computation.6 | async-start | bytes 4866048 | tf_op jit(solution)/shard_map/all_gather | solution.py:206
  9.4 251.2 %all-gather.11.cloned.1.call-start = ((), (), s32[]{:S(2)}) async-start(), calls=%async_computation.7 | async-start | bytes 4866048 | tf_op jit(solution)/shard_map/all_gather | solution.py:208
  10.0 417.9 %reduce-scatter.7.cloned.1.call-start = ((), (), s32[]{:S(2)}) async-start(), calls=%async_computation.9 | async-start | bytes 2433024 | tf_op jit(solution)/shard_map/reduce_scatter | solution.py:257
  95.8 3.8 copy-start.3
  99.6 30.2 %copy-start.1 = (bf16[4,196,768]{2,0,1:T(4,128)(2,1)S(1)}, bf16[4,196,768]{2,0,1:T(4,128)(2,1)}, u32[]{:S(2)}) copy-start(bf16[4,196,768]{2,0,1:T(4,128)(2,1)} %param.16) | copy-start | bytes 3612676
  133.1 1.5 copy-start.5
  204.9 3.7 copy-start.4
  208.6 52.0 %copy-start.9 = (bf16[4,196,768]{2,0,1:T(4,128)(2,1)S(1)}, bf16[4,196,768]{2,0,1:T(4,128)(2,1)}, u32[]{:S(2)}) copy-start(bf16[4,196,768]{2,0,1:T(4,128)(2,1)} %param.17) | copy-start | bytes 3612676
  260.6 12.6 %copy-start.6 = (f32[4,196,768]{2,1,0:T(8,128)S(1)}, f32[4,196,768]{2,1,0:T(8,128)}, u32[]{:S(2)}) copy-start(f32[4,196,768]{2,1,0:T(8,128)} %copy-done.5) | copy-start | bytes 7225348
  273.2 8.7 %copy-start.14 = (bf16[4,196,3072]{2,1,0:T(8,128)(2,1)}, bf16[4,196,3072]{2,1,0:T(8,128)(2,1)S(1)}, u32[]{:S(2)}) copy-start(bf16[4,196,3072]{2,1,0:T(8,128)(2,1)S(1)} %get-tuple-element.107) | copy-start | bytes 14450692
  281.9 2.6 copy-start.13
  283.0 1.4 copy-start.2
  283.0 4.3 copy-start.12
  301.2 223.3 %reduce-scatter.5.cloned.1.call-start = ((), (), s32[]{:S(2)}) async-start(), calls=%async_computation.8 | async-start | bytes 7299072 | tf_op jit(solution)/shard_map/reduce_scatter | solution.py:254
  312.8 4.8 copy-start
  327.7 2.2 copy-start.8
  336.7 328.9 %reduce-scatter.9.cloned.1.call-start = ((), (), s32[]{:S(2)}) async-start(), calls=%async_computation.10 | async-start | bytes 9732096 | tf_op jit(solution)/shard_map/reduce_scatter | solution.py:239
  347.3 1.5 copy-start.10
  347.3 460.6 %reduce-scatter.11.cloned.1.call-start = ((), (), s32[]{:S(2)}) async-start(), calls=%async_computation.11 | async-start | bytes 9732096 | tf_op jit(solution)/shard_map/reduce_scatter | solution.py:241
  358.6 0.7 copy-start.11
  413.6 5.6 slice-start
  413.6 5.6 copy-start.7
  413.6 5.6 slice-start.1
Sparse Core Ops, SparseCore 0:
  10.9 62.9 all-gather.4
  76.8 52.9 all-gather.6
  132.7 62.5 all-gather.8
  198.1 62.4 all-gather.10
  301.3 97.8 reduce-scatter.6
  406.3 118.1 reduce-scatter.4
  531.0 134.6 reduce-scatter.8
  673.1 134.7 reduce-scatter.10
where the time goes:
time: 822 us; the launch traced here: 815 us
  waiting for transfers between devices  507 us (62%)
  matrix products  119 us (14%)
  blocking collectives  83.7 us (10%)
  other arithmetic  49.8 us (6%)
  local copies, waits for them, and re-layouts  39.7 us (5%)
  between operations  14.6 us (2%)
    reduce_scatter x1, waiting for transfers between devices, shards(): lax.psum_scatter(down_grad, 'fsdp', scatter_dimension=1, tiled=True)  142 us
    reduce_scatter x1, waiting for transfers between devices, shards(): lax.psum_scatter(up_grad, 'fsdp', scatter_dimension=1, tiled=True)  141 us
    reduce_scatter x1, waiting for transfers between devices, shards(): lax.psum_scatter(qkv_grad, 'fsdp', scatter_dimension=1, tiled=True)  96.6 us
    unnamed x2, blocking collectives  83.7 us
    all_gather x1, waiting for transfers between devices, shards(): lax.all_gather(up_weight, 'fsdp', axis=1, tiled=True)  60.3 us
    unnamed x64, local copies, waits for them, and re-layouts  30.9 us
    dot_general x4, matrix products, cross_rows(): jnp.einsum('gsd,gse->de', left, right, preferred_element_type=jnp.float32)  30 us
    all_gather x1, waiting for transfers between devices, shards(): lax.all_gather(down_weight, 'fsdp', axis=1, tiled=True)  28.3 us
  transfers between devices with their start and end apart: 8, of which 7 were waited for; matrix products, arithmetic and copies ran while one was open for 19% of the time, Pallas kernels for 0%

commit v1 on v0

v1 whole, which is shorter than its diff:
```python
import functools

import jax
import jax.numpy as jnp
from jax import lax
from jax.experimental import pallas as pl
from jax.experimental.pallas import tpu as pltpu
from jax.sharding import PartitionSpec as P

H = 12
HD = 64
EPS = 1e-06
BF = jnp.bfloat16
F32 = jnp.float32
VMEM_LIMIT = 56 * 1024 * 1024
CHUNKS = 2


def dot(left, right, left_dim, right_dim):
    return lax.dot_general(
        left, right, (((left_dim,), (right_dim,)), ((), ())), preferred_element_type=F32
    )


def norm_parts(values):
    center = values - jnp.mean(values, axis=-1, keepdims=True)
    rscale = lax.rsqrt(jnp.mean(center * center, axis=-1, keepdims=True) + EPS)
    return center * rscale, rscale


def norm_back(grad_normal, normal, rscale):
    grad_mean = jnp.mean(grad_normal, axis=-1, keepdims=True)
    grad_cross = jnp.mean(grad_normal * normal, axis=-1, keepdims=True)
    return rscale * (grad_normal - grad_mean - normal * grad_cross)


def gelu_parts(values):
    size = jnp.abs(values)
    step = 1.0 / (1.0 + (0.3275911 * 0.7071067811865476) * size)
    bell = jnp.exp(-0.5 * values * values)
    poly = 1.061405429 * 0.5
    for factor in (-1.453152027, 1.421413741, -0.284496736, 0.254829592):
        poly = poly * step + 0.5 * factor
    tail = poly * step * bell
    return jnp.where(values >= 0, 1.0 - tail, tail), values * bell * 0.3989422804014327


def params(**more):
    return pltpu.CompilerParams(vmem_limit_bytes=VMEM_LIMIT, **more)


def cost(flops, moved):
    return pl.CostEstimate(flops=flops, bytes_accessed=moved, transcendentals=0)


def qkv_body(tokens, vectors, bias, weight, normed, qkv):
    @pl.when(pl.program_id(0) == 0)
    def first():
        rows = normed.shape[0] // 13

        def block(index, carry):
            at = pl.ds(pl.multiple_of(index * rows, rows), rows)
            normal, _ = norm_parts(tokens[at, :].astype(F32))
            normed[at, :] = (normal * vectors[0:1, :] + vectors[1:2, :]).astype(BF)
            return carry

        lax.fori_loop(0, 13, block, 0)

    qkv[...] = (dot(normed[...], weight[...], 1, 1) + bias[...]).astype(BF)


def qkv_call(tokens, vectors, bias, weight):
    rows, width = tokens.shape
    return pl.pallas_call(
        qkv_body,
        grid=(3,),
        in_specs=[
            pl.BlockSpec((rows, width), lambda j: (0, 0)),
            pl.BlockSpec((8, width), lambda j: (0, 0)),
            pl.BlockSpec((1, width), lambda j: (0, j)),
            pl.BlockSpec((width, width), lambda j: (j, 0)),
        ],
        out_specs=[
            pl.BlockSpec((rows, width), lambda j: (0, 0)),
            pl.BlockSpec((rows, width), lambda j: (0, j)),
        ],
        out_shape=[
            jax.ShapeDtypeStruct((rows, width), BF),
            jax.ShapeDtypeStruct((rows, 3 * width), BF),
        ],
        compiler_params=params(),
        cost_estimate=cost(6 * rows * width * width, 2 * (5 * rows * width + 3 * width * width)),
        name="qkv",
    )(tokens, vectors, bias, weight)


def attend_body(lengths, qkv, tokens, vectors, weight, mixture, middle, normed):
    slots, width = tokens.shape
    live = lax.broadcasted_iota(jnp.int32, (slots, slots), 1) < lengths[pl.program_id(0)]
    near = lax.broadcasted_iota(jnp.int32, (slots, 2 * HD), 1) < HD
    for pair in range(H // 2):
        at = 2 * HD * pair
        query = qkv[:, at : at + 2 * HD] * HD**-0.5
        key = qkv[:, width + at : width + at + 2 * HD]
        value = qkv[:, 2 * width + at : 2 * width + at + 2 * HD]
        mixed = []
        for half in (near, ~near):
            scores = dot(jnp.where(half, query, 0), key, 1, 1)
            scores = jnp.where(live, scores, -1e30)
            powers = jnp.exp(scores - jnp.max(scores, axis=1, keepdims=True))
            weights = powers * (1.0 / jnp.sum(powers, axis=1, keepdims=True))
            mixed.append(dot(weights.astype(BF), value, 1, 0))
        mixture[:, at : at + 2 * HD] = jnp.where(near, mixed[0], mixed[1]).astype(BF)
    branch = dot(mixture[...], weight[...], 1, 1)
    middle[...] = branch + (tokens[...].astype(F32) + vectors[4:5, :])
    normal, _ = norm_parts(middle[...])
    normed[...] = (normal * vectors[5:6, :] + vectors[6:7, :]).astype(BF)


def attend_call(lengths, qkv, tokens, vectors, weight):
    rows, width = tokens.shape
    images = lengths.shape[0]
    slots = rows // images
    row = pl.BlockSpec((slots, width), lambda i, *_: (i, 0))
    return pl.pallas_call(
        attend_body,
        grid_spec=pltpu.PrefetchScalarGridSpec(
            num_scalar_prefetch=1,
            grid=(images,),
            in_specs=[
                pl.BlockSpec((slots, 3 * width), lambda i, *_: (i, 0)),
                row,
                pl.BlockSpec((8, width), lambda i, *_: (0, 0)),
                pl.BlockSpec((width, width), lambda i, *_: (0, 0)),
            ],
            out_specs=[row, row, row],
        ),
        out_shape=[
            jax.ShapeDtypeStruct((rows, width), BF),
            jax.ShapeDtypeStruct((rows, width), F32),
            jax.ShapeDtypeStruct((rows, width), BF),
        ],
        compiler_params=params(),
        cost_estimate=cost(16 * rows * width * width, 16 * rows * width),
        name="attend",
    )(lengths, qkv, tokens, vectors, weight)


def feed_body(hops, *refs):
    if hops:
        table, normed, cot, up, down, bias, feed, back, bias_grad = refs[:9]
        groups, hidden, slope, held = refs[9:13], refs[13], refs[14], refs[15]
    else:
        normed, cot, up, down, bias, feed, back, bias_grad, up_grad, down_grad, hidden, slope = refs
    step = pl.program_id(0)
    slots = normed.shape[0] // 4
    total = jnp.zeros_like(bias_grad)
    for part in range(4):
        at = slice(slots * part, slots * (part + 1))
        before = dot(normed[at, :], up[...], 1, 1) + bias[...]
        grad = dot(cot[at, :], down[...], 1, 0)
        share, bend = gelu_parts(before)
        hidden[at, :] = (before * share).astype(BF)
        low = (grad * (share + bend)).astype(BF)
        slope[at, :] = low
        total += jnp.sum(low.astype(F32), axis=0, keepdims=True)
        ahead = dot(hidden[at, :], down[...], 1, 1)
        behind = dot(low, up[...], 1, 0)

        @pl.when(step == 0)
        def start():
            feed[at, :] = ahead
            back[at, :] = behind

        @pl.when(step != 0)
        def go():
            feed[at, :] += ahead
            back[at, :] += behind

    bias_grad[...] = total
    up_found = dot(slope[...], normed[...], 0, 0)
    down_found = dot(cot[...], hidden[...], 0, 0)
    if not hops:
        up_grad[...] = up_found.astype(BF)
        down_grad[...] = down_found.astype(BF)
        return
    width = normed.shape[1]
    tiles = held.shape[1] * 256 // (2 * width)
    many = width // (32 // tiles)
    for owner in range(32 // tiles):
        block = up_found[many * owner : many * (owner + 1)].reshape(many // 8, 8, width)
        held[step * (32 // tiles) + owner, : many // 8] = block.astype(BF)
    few = width // 32
    for owner in range(32):
        block = down_found[few * owner : few * (owner + 1)].reshape(few // 8, 8, width)
        held[owner, pl.ds(many // 8 + step * (few // 8), few // 8)] = block.astype(BF)

    @pl.when(step == tiles - 1)
    def last():
        deal(table, held, groups)


def feed_call(table, normed, cot, up, down, bias):
    hops = table is not None
    rows, width = normed.shape
    units = up.shape[0]
    whole = pl.BlockSpec((rows, width), lambda t, *_: (0, 0))
    tile = pl.BlockSpec((width, width), lambda t, *_: (t, 0))
    line = pl.BlockSpec((1, width), lambda t, *_: (0, t))
    scratch = [pltpu.VMEM((rows, width), BF), pltpu.VMEM((rows, width), BF)]
    if hops:
        block = 2 * units // 256
        more = [pl.BlockSpec((8, block, 8, width), lambda t, *_: (0, 0, 0, 0))] * 4
        shapes = group_shapes(block, width)
        scratch = scratch + [pltpu.VMEM((32, block, 8, width), BF)]
    else:
        more = [tile, tile]
        shapes = [jax.ShapeDtypeStruct((units, width), BF)] * 2
    return pl.pallas_call(
        functools.partial(feed_body, hops),
        grid_spec=pltpu.PrefetchScalarGridSpec(
            num_scalar_prefetch=1 if hops else 0,
            grid=(units // width,),
            in_specs=[whole, whole, tile, tile, line],
            out_specs=[whole, whole, line] + more,
            scratch_shapes=scratch,
        ),
        out_shape=[
            jax.ShapeDtypeStruct((rows, width), F32),
            jax.ShapeDtypeStruct((rows, width), F32),
            jax.ShapeDtypeStruct((1, units), F32),
        ]
        + shapes,
        compiler_params=params(),
        cost_estimate=cost(12 * rows * width * units, 20 * rows * width + 8 * units * width),
        name="feed",
    )(*(([table] if hops else []) + [normed, cot, up, down, bias]))


def close_body(count, *refs):
    middle, cot, vectors = refs[:3]
    feeds, backs = refs[3 : 3 + count], refs[3 + count : 3 + 2 * count]
    output, grad_middle, grad_low, sums = refs[3 + 2 * count :]
    slots = output.shape[1]
    total = feeds[0][...]
    behind = backs[0][...]
    for more in range(1, count):
        total += feeds[more][...]
        behind += backs[more][...]
    values = middle[...]
    given = cot[...].astype(F32)
    output[0] = (values + total + vectors[7:8, :])[:slots].astype(BF)
    normal, rscale = norm_parts(values)
    grad = given + norm_back(behind * vectors[5:6, :], normal, rscale)
    grad_middle[...] = grad
    low = grad.astype(BF)
    grad_low[...] = low

    @pl.when(pl.program_id(0) == 0)
    def start():
        sums[...] = jnp.zeros_like(sums)

    for place, term in enumerate((behind * normal, behind, given, low.astype(F32))):
        sums[place : place + 1, :] += jnp.sum(term, axis=0, keepdims=True)


def close_call(middle, cot, vectors, feeds, backs, images, slots):
    rows, width = middle.shape
    row = pl.BlockSpec((rows // images, width), lambda i: (i, 0))
    fixed = pl.BlockSpec((8, width), lambda i: (0, 0))
    return pl.pallas_call(
        functools.partial(close_body, len(feeds)),
        grid=(images,),
        in_specs=[row, row, fixed] + [row] * (2 * len(feeds)),
        out_specs=[pl.BlockSpec((1, slots, width), lambda i: (i, 0, 0)), row, row, fixed],
        out_shape=[
            jax.ShapeDtypeStruct((images, slots, width), BF),
            jax.ShapeDtypeStruct((rows, width), F32),
            jax.ShapeDtypeStruct((rows, width), BF),
            jax.ShapeDtypeStruct((8, width), F32),
        ],
        compiler_params=params(),
        cost_estimate=cost(50 * rows * width, 30 * rows * width),
        name="close",
    )(middle, cot, vectors, *feeds, *backs)


def attend_back_body(lengths, qkv, grad_low, weight, grad_qkv, grad_mix):
    slots, width = grad_low.shape
    live = lax.broadcasted_iota(jnp.int32, (slots, slots), 0) < lengths[pl.program_id(0)]
    near = lax.broadcasted_iota(jnp.int32, (slots, 2 * HD), 1) < HD
    grad_mix[...] = dot(grad_low[...], weight[...], 1, 0).astype(BF)
    for pair in range(H // 2):
        at = 2 * HD * pair
        query = qkv[:, at : at + 2 * HD] * HD**-0.5
        key = qkv[:, width + at : width + at + 2 * HD]
        value = qkv[:, 2 * width + at : 2 * width + at + 2 * HD]
        mix = grad_mix[:, at : at + 2 * HD]
        found = []
        for half in (near, ~near):
            scores = dot(key, jnp.where(half, query, 0), 1, 1)
            scores = jnp.where(live, scores, -1e30)
            powers = jnp.exp(scores - jnp.max(scores, axis=0, keepdims=True))
            weights = powers * (1.0 / jnp.sum(powers, axis=0, keepdims=True))
            slope = dot(value, jnp.where(half, mix, 0), 1, 1)
            grad_value = dot(weights.astype(BF), mix, 1, 0)
            inner = jnp.sum(slope * weights, axis=0, keepdims=True)
            low = (weights * (slope - inner)).astype(BF)
            grad_key = dot(low, query, 1, 0)
            grad_query = dot(low, key * HD**-0.5, 0, 0)
            found.append((grad_query, grad_key, grad_value))
        for place in range(3):
            grad_qkv[:, place * width + at : place * width + at + 2 * HD] = jnp.where(
                near, found[0][place], found[1][place]
            ).astype(BF)


def attend_back_call(lengths, qkv, grad_low, weight):
    rows, width = grad_low.shape
    images = lengths.shape[0]
    slots = rows // images
    wide = pl.BlockSpec((slots, 3 * width), lambda i, *_: (i, 0))
    return pl.pallas_call(
        attend_back_body,
        grid_spec=pltpu.PrefetchScalarGridSpec(
            num_scalar_prefetch=1,
            grid=(images,),
            in_specs=[
                wide,
                pl.BlockSpec((slots, width), lambda i, *_: (i, 0)),
                pl.BlockSpec((width, width), lambda i, *_: (0, 0)),
            ],
            out_specs=[wide],
            scratch_shapes=[pltpu.VMEM((slots, width), BF)],
        ),
        out_shape=[jax.ShapeDtypeStruct((rows, 3 * width), BF)],
        compiler_params=params(),
        cost_estimate=cost(30 * rows * width * width, 16 * rows * width),
        name="attend_back",
    )(lengths, qkv, grad_low, weight)[0]


def cross_flat_body(left, right, out):
    out[...] = dot(left[...], right[...], 0, 0).astype(BF)


def cross_flat_call(left, right):
    rows, width = right.shape
    wide = left.shape[1]
    return pl.pallas_call(
        cross_flat_body,
        grid=(wide // width,),
        in_specs=[
            pl.BlockSpec((rows, width), lambda j: (0, j)),
            pl.BlockSpec((rows, width), lambda j: (0, 0)),
        ],
        out_specs=pl.BlockSpec((width, width), lambda j: (j, 0)),
        out_shape=jax.ShapeDtypeStruct((wide, width), BF),
        compiler_params=params(),
        cost_estimate=cost(2 * rows * width * wide, 2 * rows * (width + wide) + 2 * wide * width),
        name="cross",
    )(left, right)


def deal(table, held, groups):
    for index in range(32):
        groups[index // 8][index % 8] = held[table[index]]


def group_shapes(units, width):
    return [jax.ShapeDtypeStruct((8, units, 8, width), BF)] * 4


def cross_body(table, left, right, *refs):
    groups, whole, held = refs[:4], refs[4], refs[5]
    step = pl.program_id(0)
    steps = pl.num_programs(0)
    width = right.shape[1]
    for index in range(whole.shape[0] // width):
        @pl.when(step == index)
        def tile():
            whole[width * index : width * (index + 1), :] = dot(left[...], right[...], 0, 0)

    @pl.when(step == steps - 1)
    def last():
        units = held.shape[1]
        for owner in range(32):
            block = whole[8 * units * owner : 8 * units * (owner + 1), :]
            held[owner] = block.reshape(units, 8, width).astype(BF)
        deal(table, held, groups)


def cross_call(table, left, right):
    rows, width = right.shape
    wide = left.shape[1]
    units = wide // 256
    group = pl.BlockSpec((8, units, 8, width), lambda j, *_: (0, 0, 0, 0))
    return pl.pallas_call(
        cross_body,
        grid_spec=pltpu.PrefetchScalarGridSpec(
            num_scalar_prefetch=1,
            grid=(wide // width,),
            in_specs=[
                pl.BlockSpec((rows, width), lambda j, *_: (0, j)),
                pl.BlockSpec((rows, width), lambda j, *_: (0, 0)),
            ],
            out_specs=[group] * 4,
            scratch_shapes=[pltpu.VMEM((wide, width), F32), pltpu.VMEM((32, units, 8, width), BF)],
        ),
        out_shape=group_shapes(units, width),
        compiler_params=params(),
        cost_estimate=cost(2 * rows * width * wide, 2 * rows * (width + wide) + 2 * wide * width),
        name="cross",
    )(table, left, right)


def enter_body(tokens, grad_qkv, grad_middle, vectors, weight, grad_input, sums, bias_sum):
    slots = grad_input.shape[1]
    low = grad_qkv[...]
    grad = dot(low, weight[...], 1, 0)
    normal, rscale = norm_parts(tokens[...].astype(F32))
    full = grad_middle[...] + norm_back(grad * vectors[0:1, :], normal, rscale)
    grad_input[0] = full[:slots]

    @pl.when(pl.program_id(0) == 0)
    def start():
        sums[...] = jnp.zeros_like(sums)
        bias_sum[...] = jnp.zeros_like(bias_sum)

    sums[0:1, :] += jnp.sum(grad * normal, axis=0, keepdims=True)
    sums[1:2, :] += jnp.sum(grad, axis=0, keepdims=True)
    bias_sum[...] += jnp.sum(low.astype(F32), axis=0, keepdims=True)


def enter_call(tokens, grad_qkv, grad_middle, vectors, weight, images, slots):
    rows, width = tokens.shape
    row = pl.BlockSpec((rows // images, width), lambda i: (i, 0))
    fixed = pl.BlockSpec((8, width), lambda i: (0, 0))
    return pl.pallas_call(
        enter_body,
        grid=(images,),
        in_specs=[
            row,
            pl.BlockSpec((rows // images, 3 * width), lambda i: (i, 0)),
            row,
            fixed,
            pl.BlockSpec((3 * width, width), lambda i: (0, 0)),
        ],
        out_specs=[
            pl.BlockSpec((1, slots, width), lambda i: (i, 0, 0)),
            fixed,
            pl.BlockSpec((1, 3 * width), lambda i: (0, 0)),
        ],
        out_shape=[
            jax.ShapeDtypeStruct((images, slots, width), F32),
            jax.ShapeDtypeStruct((8, width), F32),
            jax.ShapeDtypeStruct((1, 3 * width), F32),
        ],
        compiler_params=params(),
        cost_estimate=cost(6 * rows * width * width, 20 * rows * width),
        name="enter",
    )(tokens, grad_qkv, grad_middle, vectors, weight)


ORDERS = ((8, 16, 2, 4), (16, 8, 4, 2))


def reach(order):
    return [sum(order[bit] for bit in range(4) if index >> bit & 1) for index in range(16)]


def block_table():
    me = lax.axis_index("fsdp")
    near, far = reach(ORDERS[0]), reach(ORDERS[1])
    even = jnp.array(near + [1 ^ place for place in far], jnp.int32)
    odd = jnp.array(far + [1 ^ place for place in near], jnp.int32)
    return jnp.bitwise_xor(jnp.where(me % 2 == 0, even, odd), me.astype(jnp.int32))


def swap(values, step):
    pairs = [(index, index ^ (1 if step < 0 else ORDERS[index % 2][step])) for index in range(32)]
    return lax.ppermute(values, "fsdp", pairs)


def place_body(units, table, *refs):
    groups, parts = refs[:4], refs[4:]
    for index in range(32):
        owner = table[index]
        start = 0
        for part, unit in zip(parts, units):
            part[owner] = groups[index // 8][index % 8, start : start + unit]
            start += unit


def place_call(table, groups, units):
    width = groups[0].shape[-1]
    whole = pl.BlockSpec(memory_space=pltpu.VMEM)
    return pl.pallas_call(
        functools.partial(place_body, units),
        in_specs=[pl.BlockSpec(memory_space=pltpu.SMEM)] + [whole] * 4,
        out_specs=[whole] * len(units),
        out_shape=[jax.ShapeDtypeStruct((32, unit, 8, width), BF) for unit in units],
        compiler_params=params(),
        cost_estimate=cost(0, 4 * 256 * sum(units) * width),
        name="place",
    )(table, *groups)


def sort_body(units, full, *parts):
    start = 0
    for part, unit in zip(parts, units):
        part[...] = full[:, start : start + unit]
        start += unit


def sort_call(full, units):
    count, unit, _, width = full.shape
    some = 4
    return pl.pallas_call(
        functools.partial(sort_body, units),
        grid=(count // some,),
        in_specs=[pl.BlockSpec((some, unit, 8, width), lambda i: (i, 0, 0, 0))],
        out_specs=[pl.BlockSpec((some, part, 8, width), lambda i: (i, 0, 0, 0)) for part in units],
        out_shape=[jax.ShapeDtypeStruct((count, part, 8, width), BF) for part in units],
        compiler_params=params(),
        cost_estimate=cost(0, 4 * 8 * count * unit * width),
        name="sort",
    )(full)


def gather_hops(table, parts):
    width = parts[0].shape[-1]
    units = [part.shape[0] // 8 for part in parts]
    held = jnp.concatenate(parts, axis=0).reshape(1, sum(units), 8, width)
    for step in range(3):
        held = jnp.concatenate([held, swap(held, step)], axis=0)
    across = swap(held, -1)
    late = swap(held, 3)
    late_across = swap(late, -1)
    placed = place_call(table, (held, late, across, late_across), units)
    return [part.reshape(-1, width) for part in placed]


def gather_flat(count, parts):
    width = parts[0].shape[-1]
    packed = jnp.concatenate(parts, axis=0)
    full = lax.all_gather(packed, "fsdp", axis=0, tiled=True)
    if all(part.shape[0] % 8 == 0 for part in parts):
        units = [part.shape[0] // 8 for part in parts]
        full = full.reshape(count, sum(units), 8, width)
        return [part.reshape(-1, width) for part in sort_call(full, units)]
    full = full.reshape(count, -1, width)
    found = []
    start = 0
    for part in parts:
        found.append(full[:, start : start + part.shape[0]].reshape(-1, width))
        start += part.shape[0]
    return found


def scatter_hops(groups):
    near, far, near_across, far_across = groups
    far_in = swap(far_across, -1)
    near_in = swap(near_across, -1)
    moved = swap((far.astype(F32) + far_in.astype(F32)).astype(BF), 3)
    total = near.astype(F32) + near_in.astype(F32) + moved.astype(F32)
    for step in (2, 1, 0):
        half = 1 << step
        total = total[:half] + swap(total[half:].astype(BF), step).astype(F32)
    return total.reshape(-1, near.shape[-1])


def scatter_flat(parts):
    return [lax.psum_scatter(part.astype(F32), "fsdp", scatter_dimension=0, tiled=True) for part in parts]


def scatter_vector_hops(values):
    total = values
    me = lax.axis_index("fsdp")
    for bit in (0, 1, 2, 3, 4):
        count = total.shape[0] // 2
        pairs = [(index, index ^ (1 << bit)) for index in range(32)]
        split = total.reshape(count, 2, -1)
        mine = (me >> bit) & 1
        keep = jnp.where(mine == 0, split[:, 0], split[:, 1])
        send = jnp.where(mine == 0, split[:, 1], split[:, 0])
        total = keep + lax.ppermute(send, "fsdp", pairs)
    return total.reshape(-1)


def shards(
    count,
    tokens,
    cotangent,
    lengths,
    ln1_gain,
    ln1_bias,
    qkv_weight,
    q_bias,
    v_bias,
    out_weight,
    out_bias,
    ln2_gain,
    ln2_bias,
    up_weight,
    up_bias,
    down_weight,
    down_bias,
):
    images, slots, width = tokens.shape
    hops = count == 32
    padded = -(-slots // 16) * 16
    own = width // count
    units = up_bias.shape[0] // CHUNKS
    table = block_table() if hops else None

    singles = [ln1_gain, ln1_bias, q_bias, v_bias, out_bias, ln2_gain, ln2_bias, down_bias]
    vector = jnp.concatenate(singles + [up_bias])
    extra = jnp.zeros((8, width), BF).at[0, : vector.shape[0]].set(vector)
    qkv_rows = qkv_weight.T
    out_rows = out_weight.T
    up_rows = up_weight.T.reshape(CHUNKS, units, width)
    tiles = units * count // width
    down_rows = down_weight.reshape(count, CHUNKS, units, own).transpose(1, 3, 0, 2)
    down_rows = down_rows.reshape(CHUNKS, own, tiles, width).transpose(0, 2, 1, 3)

    first = [qkv_rows, extra]
    second = [out_rows] + [up_rows[chunk] for chunk in range(CHUNKS)]
    second += [down_rows[chunk, tile] for chunk in range(CHUNKS) for tile in range(tiles)]
    if hops:
        qkv_full, extra_full = gather_hops(table, first)
    else:
        qkv_full, extra_full = gather_flat(count, first)
    rest = gather_flat(count, second)
    out_full = rest[0]
    up_full = rest[1 : 1 + CHUNKS]
    down_full = [
        jnp.concatenate(rest[1 + CHUNKS + tiles * chunk : 1 + CHUNKS + tiles * (chunk + 1)])
        for chunk in range(CHUNKS)
    ]

    extra_full = extra_full.reshape(count, 8, width)[:, 0, : vector.shape[0]].astype(F32)
    vectors = extra_full[:, : 8 * own].reshape(count, 8, own).transpose(1, 0, 2).reshape(8, width)
    up_bias_full = extra_full[:, 8 * own :].reshape(count, CHUNKS, units).transpose(1, 0, 2)
    up_bias_full = up_bias_full.reshape(CHUNKS, 1, count * units)
    qkv_bias = jnp.concatenate([vectors[2], jnp.zeros((width,), F32), vectors[3]])[None]

    pad = ((0, 0), (0, padded - slots), (0, 0))
    token_rows = jnp.pad(tokens, pad).reshape(images * padded, width)
    cot_rows = jnp.pad(cotangent, pad).reshape(images * padded, width)

    normed_one, qkv = qkv_call(token_rows, vectors, qkv_bias, qkv_full)
    mixture, middle, normed_two = attend_call(lengths, qkv, token_rows, vectors, out_full)
    feeds, backs, bias_grads, sums = [], [], [], []
    for chunk in range(CHUNKS):
        feed, back, bias_grad, *found = feed_call(
            table, normed_two, cot_rows, up_full[chunk], down_full[chunk], up_bias_full[chunk]
        )
        feeds.append(feed)
        backs.append(back)
        bias_grads.append(bias_grad)
        if hops:
            sums.append(scatter_hops(found))
        else:
            split = jnp.split(found[1], tiles)
            sums.append(jnp.concatenate(scatter_flat([found[0]] + split)))
    output, grad_middle, grad_low, close_sums = close_call(
        middle, cot_rows, vectors, feeds, backs, images, slots
    )
    if hops:
        out_sum = scatter_hops(cross_call(table, grad_low, mixture))
    else:
        (out_sum,) = scatter_flat([cross_flat_call(grad_low, mixture)])
    grad_qkv = attend_back_call(lengths, qkv, grad_low, out_full)
    if hops:
        qkv_sum = scatter_hops(cross_call(table, grad_qkv, normed_one))
    else:
        (qkv_sum,) = scatter_flat([cross_flat_call(grad_qkv, normed_one)])
    grad_input, enter_sums, qkv_bias_sum = enter_call(
        token_rows, grad_qkv, grad_middle, vectors, qkv_full, images, slots
    )

    wide = qkv_bias_sum[0]
    eight = jnp.stack(
        [
            enter_sums[0],
            enter_sums[1],
            wide[:width],
            wide[2 * width :],
            close_sums[3],
            close_sums[0],
            close_sums[1],
            close_sums[2],
        ]
    )
    eight = eight.reshape(8, count, own).transpose(1, 0, 2).reshape(count, 8 * own)
    many = jnp.stack(bias_grads).reshape(CHUNKS, count, units).transpose(1, 0, 2)
    every = jnp.concatenate([eight, many.reshape(count, CHUNKS * units)], axis=1)
    if hops:
        small = scatter_vector_hops(every)
    else:
        small = lax.psum_scatter(every.reshape(-1), "fsdp", scatter_dimension=0, tiled=True)
    vec = [small[own * place : own * (place + 1)] for place in range(8)]

    up_sum = jnp.concatenate([found[:units] for found in sums]).T
    down_sum = jnp.stack([found[units:].reshape(tiles, own, width) for found in sums])
    down_sum = down_sum.transpose(0, 2, 1, 3).reshape(CHUNKS, own, count, units)
    down_sum = down_sum.transpose(2, 0, 3, 1).reshape(count * CHUNKS * units, own)
    return (
        output,
        grad_input,
        vec[0],
        vec[1],
        qkv_sum.T,
        vec[2],
        vec[3],
        out_sum.T,
        vec[4],
        vec[5],
        vec[6],
        up_sum,
        small[8 * own :],
        down_sum,
        vec[7],
    )


def solution(mesh):
    row, column, vector = P("fsdp", None, None), P(None, "fsdp"), P("fsdp")
    return jax.shard_map(
        functools.partial(shards, mesh.shape["fsdp"]),
        mesh=mesh,
        in_specs=(row, row, vector, vector, vector, column, vector, vector, column, vector)
        + (vector, vector, column, vector, column, vector),
        out_specs=(row, row, vector, vector, column, vector, vector, column, vector)
        + (vector, vector, column, vector, column, vector),
        check_vma=False,
    )
```

time: 822 us -> 361 us (0.44)
  waiting for transfers between devices: 507 us -> 125 us
  Pallas kernels: 0 us -> 145 us
  matrix products: 119 us -> 0 us
  blocking collectives: 83.7 us -> 0 us
  other arithmetic: 49.8 us -> 11.7 us
  starting transfers between devices: 0.93 us -> 38.3 us
  local copies, waits for them, and re-layouts: 39.7 us -> 21.4 us
    reduce_scatter x4 -> x0, waiting for transfers between devices: 380 us -> none  [the longest x1 142 us: shards(): lax.psum_scatter(down_grad, 'fsdp', scatter_dimension=1, tiled=True)]
    pallas_call x0 -> x11, Pallas kernels: none -> 145 us  [the longest x2 52.5 us: feed_call(): pl.pallas_call(functools.partial(feed_body, hops), grid_spec=pltpu.Prefet...]
    dot_general x18 -> x0, matrix products: 119 us -> none  [the longest x4 30 us: cross_rows(): jnp.einsum('gsd,gse->de', left, right, preferred_element_type=jnp.float32)]
    ppermute x0 -> x35, waiting for transfers between devices: none -> 93.1 us  [the longest x30 90 us: swap(): return lax.ppermute(values, 'fsdp', pairs)]
    all_gather x4 -> x1, waiting for transfers between devices: 124 us -> 32 us  [gather_flat(): full = lax.all_gather(packed, 'fsdp', axis=0, tiled=True)]
    unnamed x2 -> x0, blocking collectives: 83.7 us -> none
    ppermute x0 -> x35, starting transfers between devices: none -> 38.3 us  [the longest x30 32.5 us: swap(): return lax.ppermute(values, 'fsdp', pairs)]
    convert_element_type x10 -> x5, other arithmetic: 35.1 us -> 1.88 us  [the longest x1 0.95 us: shards(): extra_full.reshape(count, 8, width)[:, 0, :vector.shape[0]].astype(F32)]
  transfers between devices with their start and end apart: 8 -> 36, of which waited for: 7 -> 17; matrix products, arithmetic and copies ran while one was open for 19% -> 5% of each run, Pallas kernels for 0% -> 8%
where the time goes in v1:
time: 361 us; the launch traced here: 357 us
  Pallas kernels  145 us (40%)
  waiting for transfers between devices  125 us (35%)
  starting transfers between devices  38.3 us (11%)
  local copies, waits for them, and re-layouts  21.4 us (6%)
  between operations  15.4 us (4%)
  other arithmetic  11.7 us (3%)
    ppermute x30, waiting for transfers between devices, swap(): return lax.ppermute(values, 'fsdp', pairs)  90 us
    pallas_call x2, Pallas kernels, feed_call(): pl.pallas_call(functools.partial(feed_body, hops), grid_spec=pltpu.Prefet...  52.5 us
    ppermute x30, starting transfers between devices, swap(): return lax.ppermute(values, 'fsdp', pairs)  32.5 us
    all_gather x1, waiting for transfers between devices, gather_flat(): full = lax.all_gather(packed, 'fsdp', axis=0, tiled=True)  32 us
    pallas_call x1, Pallas kernels, attend_back_call(): pl.pallas_call(attend_back_body, grid_spec=pltpu.PrefetchScalarGridSpec(n...  22.1 us
    pallas_call x2, Pallas kernels, cross_call(): pl.pallas_call(cross_body, grid_spec=pltpu.PrefetchScalarGridSpec(num_sca...  14.5 us
    pallas_call x1, Pallas kernels, attend_call(): pl.pallas_call(attend_body, grid_spec=pltpu.PrefetchScalarGridSpec(num_sc...  13.3 us
    pallas_call x1, Pallas kernels, qkv_call(): pl.pallas_call(qkv_body, grid=(3,), in_specs=[pl.BlockSpec((rows, width),...  10.3 us
  transfers between devices with their start and end apart: 36, of which 17 were waited for; matrix products, arithmetic and copies ran while one was open for 5% of the time, Pallas kernels for 8%

profile of v1, /device:TPU:0, one launch (start us, length us, event | category | flops | bytes accessed | tf_op | source)
XLA Modules:
  0.0 356.9 jit_solution(2245527388978117717)
XLA Ops:
  7.2 1.3 reshape.257
  10.6 3.1 collective-permute-start
  13.7 4.0 %collective-permute-done = bf16[1,10,8,768]{3,2,1,0:T(8,128)(2,1)S(1)} collective-permute-done((bf16[1,10,8,768]{3,2,1,0:T(8,128)(2,1)S(1)}, bf16[1,10,8,768]{3,2,1,0:T(8,128)(2,1)S(1)}, u32[]{:S(2)}, u32[]{:S(2)}) %collective-permute-start) | collective-permute-done | bytes 122912 | tf_op jit(solution)/shard_map/ppermute | solution.py:482
  17.7 2.2 collective-permute-start.1
  19.9 6.8 %collective-permute-done.1 = bf16[2,10,8,768]{3,2,1,0:T(8,128)(2,1)S(1)} collective-permute-done((bf16[2,10,8,768]{3,2,1,0:T(8,128)(2,1)S(1)}, bf16[2,10,8,768]{3,2,1,0:T(8,128)(2,1)S(1)}, u32[]{:S(2)}, u32[]{:S(2)}) %collective-permute-start.1) | collective-permute-done | bytes 245792 | tf_op jit(solution)/shard_map/ppermute | solution.py:482
  26.8 2.7 collective-permute-start.2
  29.5 6.8 %collective-permute-done.2 = bf16[4,10,8,768]{3,2,1,0:T(8,128)(2,1)S(1)} collective-permute-done((bf16[4,10,8,768]{3,2,1,0:T(8,128)(2,1)S(1)}, bf16[4,10,8,768]{3,2,1,0:T(8,128)(2,1)S(1)}, u32[]{:S(2)}, u32[]{:S(2)}) %collective-permute-start.2) | collective-permute-done | bytes 491552 | tf_op jit(solution)/shard_map/ppermute | solution.py:482
  36.4 2.5 collective-permute-start.3
  38.9 16.9 %collective-permute-done.3.refs_1_ = bf16[8,10,8,768]{3,2,1,0:T(8,128)(2,1)} collective-permute-done((bf16[8,10,8,768]{3,2,1,0:T(8,128)(2,1)S(1)}, bf16[8,10,8,768]{3,2,1,0:T(8,128)(2,1)}, u32[]{:S(2)}, u32[]{:S(2)}) %collective-permute-start.3) | collective-permute-done | bytes 983072 | tf_op jit(solution)/shard_map/ppermute | solution.py:482
  56.1 1.1 pad.12.clone
  58.9 4.3 %place.1 = (bf16[32,9,8,768]{3,2,1,0:T(8,128)(2,1)}, bf16[32,1,8,768]{3,2,1,0:T(8,128)(2,1)}) custom-call(s32[32]{0:T(128)} %fusion.18.table.refs_0_, bf16[8,10,8,768]{3,2,1,0:T(8,128)(2,1)} %copy-done, bf16[8,10,8,768]{3,2,1,0:T(8,128)(2,1)} %collective-permute-done.3.refs_1_, bf16[8,10,8,768]{3,2,1,0:T(8,128)(2,1)} %collective-permute-done.4.refs_2_, ...), custom_call_target="tpu_custom_call" | custom-call | bytes 7864320 | tf_op jit(solution)/shard_map/place/pallas_call | solution.py:498
  67.5 10.3 %qkv.1 = (bf16[832,768]{1,0:T(8,128)(2,1)}, bf16[832,2304]{1,0:T(8,128)(2,1)}) custom-call(bf16[832,768]{1,0:T(8,128)(2,1)} %bitcast.125, f32[8,768]{1,0:T(8,128)} %reshape.255.vectors.refs_2_, f32[1,2304]{1,0:T(1,128)} %broadcast_in_dim.8.bias, bf16[2304,768]{1,0:T(8,128)(2,1)} %bitcast.131), custom_call_target="tpu_custom_call" | custom-call | flops 2944401408 | bytes 9928704 | tf_op jit(solution)/shard_map/qkv/pallas_call | solution.py:74
  77.8 32.0 %all-gather.2.cloned.1.call-done = bf16[6912,768]{1,0:T(8,128)(2,1)} async-done(((bf16[216,768]{1,0:T(8,128)(2,1)}), bf16[6912,768]{1,0:T(8,128)(2,1)}) %all-gather.2.cloned.1.call-update) | async-done | bytes 10616848 | tf_op jit(solution)/shard_map/all_gather | solution.py:547
  109.7 10.2 %sort.1 = (bf16[32,3,8,768]{3,2,1,0:T(8,128)(2,1)}, bf16[32,6,8,768]{3,2,1,0:T(8,128)(2,1)}, bf16[32,6,8,768]{3,2,1,0:T(8,128)(2,1)}, bf16[32,3,8,768]{3,2,1,0:T...) custom-call(bf16[32,27,8,768]{3,2,1,0:T(8,128)(2,1)} %bitcast.124), custom_call_target="tpu_custom_call" | custom-call | bytes 21233664 | tf_op jit(solution)/shard_map/sort/pallas_call | solution.py:519
  120.0 3.3 pad_maximum_fusion.refs_4_
  123.3 1.6 pad_maximum_fusion.1.refs_4_
  124.9 13.3 %attend.1 = (bf16[832,768]{1,0:T(8,128)(2,1)}, f32[832,768]{1,0:T(8,128)}, bf16[832,768]{1,0:T(8,128)(2,1)}) custom-call(s32[4]{0:T(128)} %lengths.3, bf16[832,2304]{1,0:T(8,128)(2,1)} %get-tuple-element.72.qkv, bf16[832,768]{1,0:T(8,128)(2,1)} %bitcast.126, f32[8,768]{1,0:T(8,128)} %reshape.255.vectors.refs_2_, bf16[768,768]{1,0:T(8,128)(2,1)} %bitcast.158), custom_call_target="tpu_custom_call" | custom-call | flops 7851737088 | bytes 10223616 | tf_op jit(solution)/shard_map/attend/pallas_call | solution.py:125
  138.2 26.2 %feed.2 = (f32[832,768]{1,0:T(8,128)}, f32[832,768]{1,0:T(8,128)}, f32[1,1536]{1,0:T(1,128)}, bf16[8,12,8,768]{3,2,1,0:T(8,128)(2,1)}, bf16[8,12,8,768]{3,2,1,0:...) custom-call(s32[32]{0:T(128)} %fusion.18.table.refs_0_, ...), custom_call_target="tpu_custom_call" | custom-call | flops 11777605632 | bytes 22216704 | tf_op jit(solution)/shard_map/feed/pallas_call | solution.py:219
  164.4 26.3 %feed.3 = (f32[832,768]{1,0:T(8,128)}, f32[832,768]{1,0:T(8,128)}, f32[1,1536]{1,0:T(1,128)}, bf16[8,12,8,768]{3,2,1,0:T(8,128)(2,1)}, bf16[8,12,8,768]{3,2,1,0:...) custom-call(s32[32]{0:T(128)} %fusion.18.table.refs_0_, ...), custom_call_target="tpu_custom_call" | custom-call | flops 11777605632 | bytes 22216704 | tf_op jit(solution)/shard_map/feed/pallas_call | solution.py:219
  190.7 8.3 %close.1 = (bf16[4,196,768]{2,1,0:T(8,128)(2,1)}, f32[832,768]{1,0:T(8,128)}, bf16[832,768]{1,0:T(8,128)(2,1)}, f32[8,768]{1,0:T(8,128)}) custom-call(f32[832,768]{1,0:T(8,128)} %get-tuple-element.74.refs_0_, bf16[832,768]{1,0:T(8,128)(2,1)} %bitcast.130, f32[8,768]{1,0:T(8,128)} %reshape.255.vectors.refs_2_, f32[832,768]{1,0:T(8,128)} %get-tuple-element.79.refs_3_, ...), custom_call_target="tpu_custom_call" | custom-call | flops 31948800 | bytes 19169280 | tf_op jit(solution)/shard_map/close/pallas_call | solution.py:271
  200.5 22.1 %attend_back.1.grad_qkv.left = bf16[832,2304]{1,0:T(8,128)(2,1)} custom-call(s32[4]{0:T(128)} %lengths.3, bf16[832,2304]{1,0:T(8,128)(2,1)} %get-tuple-element.72.qkv, bf16[832,768]{1,0:T(8,128)(2,1)} %get-tuple-element.87.grad_low.left, bf16[768,768]{1,0:T(8,128)(2,1)} %bitcast.159), custom_call_target="tpu_custom_call" | custom-call | flops 14722007040 | bytes 10223616 | tf_op jit(solution)/shard_map/attend_back/pallas_call | solution.py:323
  222.7 9.4 %enter.1 = (f32[4,196,768]{2,1,0:T(8,128)}, f32[8,768]{1,0:T(8,128)}, f32[1,2304]{1,0:T(1,128)}) custom-call(bf16[832,768]{1,0:T(8,128)(2,1)} %bitcast.127, bf16[832,2304]{1,0:T(8,128)(2,1)} %attend_back.1.grad_qkv.left, f32[832,768]{1,0:T(8,128)} %get-tuple-element.88.grad_middle, f32[8,768]{1,0:T(8,128)} %reshape.255.vectors.refs_2_, ...), custom_call_target="tpu_custom_call" | custom-call | flops 2944401408 | bytes 12779520 | tf_op jit(solution)/shard_map/enter/pallas_call | solution.py:439
  236.1 1.6 collective-permute-start.7
  237.8 2.1 collective-permute-done.7
  239.9 1.8 collective-permute-start.8
  241.7 4.8 %cross.3 = (bf16[8,3,8,768]{3,2,1,0:T(8,128)(2,1)}, bf16[8,3,8,768]{3,2,1,0:T(8,128)(2,1)}, bf16[8,3,8,768]{3,2,1,0:T(8,128)(2,1)}, bf16[8,3,8,768]{3,2,1,0:T(8,128)(2,1)}) custom-call(s32[32]{0:T(128)} %fusion.18.table.refs_0_, bf16[832,768]{1,0:T(8,128)(2,1)} %get-tuple-element.87.grad_low.left, bf16[832,768]{1,0:T(8,128)(2,1)} %get-tuple-element.100.right), custom_call_target="tpu_custom_call" | custom-call | flops 981467136 | bytes 3735552 | tf_op jit(solution)/shard_map/cross/pallas_call | solution.py:398
  248.1 9.7 %cross.2 = (bf16[8,9,8,768]{3,2,1,0:T(8,128)(2,1)}, bf16[8,9,8,768]{3,2,1,0:T(8,128)(2,1)}, bf16[8,9,8,768]{3,2,1,0:T(8,128)(2,1)}, bf16[8,9,8,768]{3,2,1,0:T(8,128)(2,1)}) custom-call(s32[32]{0:T(128)} %fusion.18.table.refs_0_, bf16[832,2304]{1,0:T(8,128)(2,1)} %attend_back.1.grad_qkv.left, bf16[832,768]{1,0:T(8,128)(2,1)} %get-tuple-element.95.right), custom_call_target="tpu_custom_call" | custom-call | flops 2944401408 | bytes 8650752 | tf_op jit(solution)/shard_map/cross/pallas_call | solution.py:398
  259.8 2.4 copy.104
  262.2 1.5 copy.103
  264.9 1.3 collective-permute-start.20
  267.9 3.1 collective-permute-done.20
  272.0 2.0 collective-permute-start.25
  274.3 1.7 collective-permute-start.21
  276.0 3.6 collective-permute-done.13
  280.7 1.4 collective-permute-start.14
  282.7 11.1 %collective-permute-done.14 = bf16[4,9,8,768]{3,2,1,0:T(8,128)(2,1)S(1)} collective-permute-done((bf16[4,9,8,768]{3,2,1,0:T(8,128)(2,1)S(1)}, bf16[4,9,8,768]{3,2,1,0:T(8,128)(2,1)S(1)}, u32[]{:S(2)}, u32[]{:S(2)}) %collective-permute-start.14) | collective-permute-done | bytes 442400 | tf_op jit(solution)/shard_map/ppermute | solution.py:482
  293.9 1.2 collective-permute-start.22
  295.2 1.6 collective-permute-start.15
  297.4 1.3 collective-permute-start.26
  298.7 17.2 %collective-permute-done.31 = bf16[8,12,8,768]{3,2,1,0:T(8,128)(2,1)S(1)} collective-permute-done((bf16[8,12,8,768]{3,2,1,0:T(8,128)(2,1)S(1)}, bf16[8,12,8,768]{3,2,1,0:T(8,128)(2,1)S(1)}, u32[]{:S(2)}, u32[]{:S(2)}) %collective-permute-start.31) | collective-permute-done | bytes 1179680 | tf_op jit(solution)/shard_map/ppermute | solution.py:482
  318.0 1.2 collective-permute-start.16
  319.3 1.5 collective-permute-start.27
  320.8 5.5 %collective-permute-done.32 = bf16[4,12,8,768]{3,2,1,0:T(8,128)(2,1)S(1)} collective-permute-done((bf16[4,12,8,768]{3,2,1,0:T(8,128)(2,1)S(1)}, bf16[4,12,8,768]{3,2,1,0:T(8,128)(2,1)S(1)}, u32[]{:S(2)}, u32[]{:S(2)}) %collective-permute-start.32) | collective-permute-done | bytes 589856 | tf_op jit(solution)/shard_map/ppermute | solution.py:482
  326.5 1.7 collective-permute-start.33
  329.7 2.2 collective-permute-start.28
  331.9 8.5 %collective-permute-done.33 = bf16[2,12,8,768]{3,2,1,0:T(8,128)(2,1)S(1)} collective-permute-done((bf16[2,12,8,768]{3,2,1,0:T(8,128)(2,1)S(1)}, bf16[2,12,8,768]{3,2,1,0:T(8,128)(2,1)S(1)}, u32[]{:S(2)}, u32[]{:S(2)}) %collective-permute-start.33) | collective-permute-done | bytes 294944 | tf_op jit(solution)/shard_map/ppermute | solution.py:482
  340.8 5.0 %collective-permute-done.34 = bf16[1,12,8,768]{3,2,1,0:T(8,128)(2,1)S(1)} collective-permute-done((bf16[1,12,8,768]{3,2,1,0:T(8,128)(2,1)S(1)}, bf16[1,12,8,768]{3,2,1,0:T(8,128)(2,1)S(1)}, u32[]{:S(2)}, u32[]{:S(2)}) %collective-permute-start.34) | collective-permute-done | bytes 147488 | tf_op jit(solution)/shard_map/ppermute | solution.py:482
  347.2 1.8 reshape.276
  (235 shorter events, 29.9 us)
Async XLA Ops:
  7.2 102.5 %all-gather.2.cloned.1.call-start = ((), (), s32[]{:S(2)}) async-start(), calls=%async_computation | async-start | bytes 10948608 | tf_op jit(solution)/shard_map/all_gather | solution.py:547
  10.6 7.1 %collective-permute-start = (bf16[1,10,8,768]{3,2,1,0:T(8,128)(2,1)S(1)}, bf16[1,10,8,768]{3,2,1,0:T(8,128)(2,1)S(1)}, u32[]{:S(2)}, u32[]{:S(2)}) collective-permute-start(bf16[1,10,8,768]{3,2,1,0:T(8,128)(2,1)S(1)} %fusion.3), channel_id=1, source_target_pairs={{0,8},{1,17},{2,10},{3,19},{4,12},{5,21},{6,14},{7,23},{8,0},{9,25... | collective-permute-start | bytes 368648 | tf_op jit(solution)/shard_map/ppermute | solution.py:482
  17.7 38.1 %copy-start.3 = (bf16[4,196,768]{2,0,1:T(4,128)(2,1)S(1)}, bf16[4,196,768]{2,0,1:T(4,128)(2,1)}, u32[]{:S(2)}) copy-start(bf16[4,196,768]{2,0,1:T(4,128)(2,1)} %param.20) | copy-start | bytes 3612676
  17.7 9.0 %collective-permute-start.1 = (bf16[2,10,8,768]{3,2,1,0:T(8,128)(2,1)S(1)}, bf16[2,10,8,768]{3,2,1,0:T(8,128)(2,1)S(1)}, u32[]{:S(2)}, u32[]{:S(2)}) collective-permute-start(bf16[2,10,8,768]{3,2,1,0:T(8,128)(2,1)S(1)} %pad_maximum_fusion.4), channel_id=1, source_target_pairs={{0,16},{1,9},{2,18},{3,11},{4,20},{5,13},{6,22},{7,15},{8,24},{9,1... | collective-permute-start | bytes 737288 | tf_op jit(solution)/shard_map/ppermute | solution.py:482
  26.8 9.5 %collective-permute-start.2 = (bf16[4,10,8,768]{3,2,1,0:T(8,128)(2,1)S(1)}, bf16[4,10,8,768]{3,2,1,0:T(8,128)(2,1)S(1)}, u32[]{:S(2)}, u32[]{:S(2)}) collective-permute-start(bf16[4,10,8,768]{3,2,1,0:T(8,128)(2,1)S(1)} %pad_maximum_fusion.3), channel_id=1, source_target_pairs={{0,2},{1,5},{2,0},{3,7},{4,6},{5,1},{6,4},{7,3},{8,10},{9,13},{10,... | collective-permute-start | bytes 1474568 | tf_op jit(solution)/shard_map/ppermute | solution.py:482
  36.4 19.7 %copy-start = (bf16[8,10,8,768]{3,2,1,0:T(8,128)(2,1)}, bf16[8,10,8,768]{3,2,1,0:T(8,128)(2,1)S(1)}, u32[]{:S(2)}) copy-start(bf16[8,10,8,768]{3,2,1,0:T(8,128)(2,1)S(1)} %pad_maximum_fusion.2.refs_0_) | copy-start | bytes 2949124
  36.4 19.5 %copy-start.4 = (bf16[4,196,768]{2,0,1:T(4,128)(2,1)S(1)}, bf16[4,196,768]{2,0,1:T(4,128)(2,1)}, u32[]{:S(2)}) copy-start(bf16[4,196,768]{2,0,1:T(4,128)(2,1)} %param.21) | copy-start | bytes 3612676
  36.4 19.4 %collective-permute-start.3 = (bf16[8,10,8,768]{3,2,1,0:T(8,128)(2,1)S(1)}, bf16[8,10,8,768]{3,2,1,0:T(8,128)(2,1)}, u32[]{:S(2)}, u32[]{:S(2)}) collective-permute-start(bf16[8,10,8,768]{3,2,1,0:T(8,128)(2,1)S(1)} %pad_maximum_fusion.2.refs_0_), channel_id=1, source_target_pairs={{0,4},{1,3},{2,6},{3,1},{4,0},{5,7},{6,2},{7,5},{8,12},{9,11},{10,... | collective-permute-start | bytes 2949128 | tf_op jit(solution)/shard_map/ppermute | solution.py:482
  38.9 20.0 %collective-permute-start.4 = (bf16[8,10,8,768]{3,2,1,0:T(8,128)(2,1)S(1)}, bf16[8,10,8,768]{3,2,1,0:T(8,128)(2,1)}, u32[]{:S(2)}, u32[]{:S(2)}) collective-permute-start(bf16[8,10,8,768]{3,2,1,0:T(8,128)(2,1)S(1)} %pad_maximum_fusion.2.refs_0_), channel_id=1, source_target_pairs={{0,1},{1,0},{2,3},{3,2},{4,5},{5,4},{6,7},{7,6},{8,9},{9,8},{10,11... | collective-permute-start | bytes 2949128 | tf_op jit(solution)/shard_map/ppermute | solution.py:482
  55.8 3.1 collective-permute-start.5
  222.7 11.6 %copy-start.20 = (f32[1,1536]{1,0:T(1,128)S(1)}, f32[1,1536]{1,0:T(1,128)}, u32[]{:S(2)}) copy-start(f32[1,1536]{1,0:T(1,128)} %get-tuple-element.94) | copy-start | bytes 18436
  222.7 11.7 %copy-start.19 = (f32[1,1536]{1,0:T(1,128)S(1)}, f32[1,1536]{1,0:T(1,128)}, u32[]{:S(2)}) copy-start(f32[1,1536]{1,0:T(1,128)} %get-tuple-element.93) | copy-start | bytes 18436
  234.8 1.3 collective-permute-start.6
  236.1 3.8 %collective-permute-start.7 = (f32[8,288]{1,0:T(8,128)S(1)}, f32[8,288]{1,0:T(8,128)S(1)}, u32[]{:S(2)}, u32[]{:S(2)}) collective-permute-start(f32[8,288]{1,0:T(8,128)S(1)} %bitcast.152), channel_id=1, source_target_pairs={{0,2},{1,3},{2,0},{3,1},{4,6},{5,7},{6,4},{7,5},{8,10},{9,11},{10,... | collective-permute-start | bytes 27656 | tf_op jit(solution)/shard_map/ppermute | solution.py:587
  239.9 7.1 %collective-permute-start.8 = (f32[4,288]{1,0:T(4,128)S(1)}, f32[4,288]{1,0:T(4,128)S(1)}, u32[]{:S(2)}, u32[]{:S(2)}) collective-permute-start(f32[4,288]{1,0:T(4,128)S(1)} %bitcast.154), channel_id=1, source_target_pairs={{0,4},{1,5},{2,6},{3,7},{4,0},{5,1},{6,2},{7,3},{8,12},{9,13},{10,... | collective-permute-start | bytes 13832 | tf_op jit(solution)/shard_map/ppermute | solution.py:587
  246.5 11.3 %collective-permute-start.18 = (bf16[8,3,8,768]{3,2,1,0:T(8,128)(2,1)}, bf16[8,3,8,768]{3,2,1,0:T(8,128)(2,1)S(1)}, u32[]{:S(2)}, u32[]{:S(2)}) collective-permute-start(bf16[8,3,8,768]{3,2,1,0:T(8,128)(2,1)} %get-tuple-element.104), channel_id=1, source_target_pairs={{0,1},{1,0},{2,3},{3,2},{4,5},{5,4},{6,7},{7,6},{8,9},{9,8},{10,11... | collective-permute-start | bytes 884744 | tf_op jit(solution)/shard_map/ppermute | solution.py:482
  246.6 17.5 %collective-permute-start.17 = (bf16[8,3,8,768]{3,2,1,0:T(8,128)(2,1)}, bf16[8,3,8,768]{3,2,1,0:T(8,128)(2,1)S(1)}, u32[]{:S(2)}, u32[]{:S(2)}) collective-permute-start(bf16[8,3,8,768]{3,2,1,0:T(8,128)(2,1)} %get-tuple-element.102), channel_id=1, source_target_pairs={{0,1},{1,0},{2,3},{3,2},{4,5},{5,4},{6,7},{7,6},{8,9},{9,8},{10,11... | collective-permute-start | bytes 884744 | tf_op jit(solution)/shard_map/ppermute | solution.py:482
  247.1 10.7 %collective-permute-start.9 = (f32[2,288]{1,0:T(2,128)S(1)}, f32[2,288]{1,0:T(2,128)S(1)}, u32[]{:S(2)}, u32[]{:S(2)}) collective-permute-start(f32[2,288]{1,0:T(2,128)S(1)} %bitcast.155), channel_id=1, source_target_pairs={{0,8},{1,9},{2,10},{3,11},{4,12},{5,13},{6,14},{7,15},{8,0},{9,1},... | collective-permute-start | bytes 6920 | tf_op jit(solution)/shard_map/ppermute | solution.py:587
  248.1 9.8 %copy-start.14 = (bf16[8,3,8,768]{3,2,1,0:T(8,128)(2,1)S(1)}, bf16[8,3,8,768]{3,2,1,0:T(8,128)(2,1)}, u32[]{:S(2)}) copy-start(bf16[8,3,8,768]{3,2,1,0:T(8,128)(2,1)} %get-tuple-element.103) | copy-start | bytes 884740
  248.1 11.6 %copy-start.34 = (bf16[8,12,8,768]{3,2,1,0:T(8,128)(2,1)S(1)}, bf16[8,12,8,768]{3,2,1,0:T(8,128)(2,1)}, u32[]{:S(2)}) copy-start(bf16[8,12,8,768]{3,2,1,0:T(8,128)(2,1)} %get-tuple-element.108) | copy-start | bytes 3538948
  248.1 11.7 %copy-start.1 = (f32[4,196,768]{2,1,0:T(8,128)S(1)}, f32[4,196,768]{2,1,0:T(8,128)}, u32[]{:S(2)}) copy-start(f32[4,196,768]{2,1,0:T(8,128)} %get-tuple-element.144) | copy-start | bytes 7225348
  257.8 8.4 %collective-permute-start.12 = (bf16[8,9,8,768]{3,2,1,0:T(8,128)(2,1)}, bf16[8,9,8,768]{3,2,1,0:T(8,128)(2,1)S(1)}, u32[]{:S(2)}, u32[]{:S(2)}) collective-permute-start(bf16[8,9,8,768]{3,2,1,0:T(8,128)(2,1)} %get-tuple-element.99), channel_id=1, source_target_pairs={{0,1},{1,0},{2,3},{3,2},{4,5},{5,4},{6,7},{7,6},{8,9},{9,8},{10,11... | collective-permute-start | bytes 2654216 | tf_op jit(solution)/shard_map/ppermute | solution.py:482
  258.0 6.8 %collective-permute-start.19 = (bf16[8,3,8,768]{3,2,1,0:T(8,128)(2,1)S(1)}, bf16[8,3,8,768]{3,2,1,0:T(8,128)(2,1)S(1)}, u32[]{:S(2)}, u32[]{:S(2)}) collective-permute-start(bf16[8,3,8,768]{3,2,1,0:T(8,128)(2,1)S(1)} %add_convert_fusion.3), channel_id=1, source_target_pairs={{0,4},{1,3},{2,6},{3,1},{4,0},{5,7},{6,2},{7,5},{8,12},{9,11},{10,... | collective-permute-start | bytes 884744 | tf_op jit(solution)/shard_map/ppermute | solution.py:482
  258.6 5.1 %collective-permute-start.10 = (f32[1,288]{1,0:T(1,128)S(1)}, f32[1,288]{1,0:T(1,128)S(1)}, u32[]{:S(2)}, u32[]{:S(2)}) collective-permute-start(f32[1,288]{1,0:T(1,128)S(1)} %fusion.17), channel_id=1, source_target_pairs={{0,16},{1,17},{2,18},{3,19},{4,20},{5,21},{6,22},{7,23},{8,24},{9,... | collective-permute-start | bytes 3464 | tf_op jit(solution)/shard_map/ppermute | solution.py:587
  259.7 11.4 %collective-permute-start.24 = (bf16[8,12,8,768]{3,2,1,0:T(8,128)(2,1)S(1)}, bf16[8,12,8,768]{3,2,1,0:T(8,128)(2,1)S(1)}, u32[]{:S(2)}, u32[]{:S(2)}) collective-permute-start(bf16[8,12,8,768]{3,2,1,0:T(8,128)(2,1)S(1)} %copy-done.34), channel_id=1, source_target_pairs={{0,1},{1,0},{2,3},{3,2},{4,5},{5,4},{6,7},{7,6},{8,9},{9,8},{10,11... | collective-permute-start | bytes 3538952 | tf_op jit(solution)/shard_map/ppermute | solution.py:482
  263.7 8.3 %collective-permute-start.30 = (bf16[8,12,8,768]{3,2,1,0:T(8,128)(2,1)S(1)}, bf16[8,12,8,768]{3,2,1,0:T(8,128)(2,1)S(1)}, u32[]{:S(2)}, u32[]{:S(2)}) collective-permute-start(bf16[8,12,8,768]{3,2,1,0:T(8,128)(2,1)S(1)} %copy-done.35), channel_id=1, source_target_pairs={{0,1},{1,0},{2,3},{3,2},{4,5},{5,4},{6,7},{7,6},{8,9},{9,8},{10,11... | collective-permute-start | bytes 3538952 | tf_op jit(solution)/shard_map/ppermute | solution.py:482
  264.1 10.2 %collective-permute-start.11 = (bf16[8,9,8,768]{3,2,1,0:T(8,128)(2,1)S(1)}, bf16[8,9,8,768]{3,2,1,0:T(8,128)(2,1)S(1)}, u32[]{:S(2)}, u32[]{:S(2)}) collective-permute-start(bf16[8,9,8,768]{3,2,1,0:T(8,128)(2,1)S(1)} %copy-done.36), channel_id=1, source_target_pairs={{0,1},{1,0},{2,3},{3,2},{4,5},{5,4},{6,7},{7,6},{8,9},{9,8},{10,11... | collective-permute-start | bytes 2654216 | tf_op jit(solution)/shard_map/ppermute | solution.py:482
  264.8 6.3 %copy-start.33 = (bf16[8,12,8,768]{3,2,1,0:T(8,128)(2,1)S(1)}, bf16[8,12,8,768]{3,2,1,0:T(8,128)(2,1)}, u32[]{:S(2)}) copy-start(bf16[8,12,8,768]{3,2,1,0:T(8,128)(2,1)} %get-tuple-element.106) | copy-start | bytes 3538948
  264.9 6.1 %collective-permute-start.20 = (bf16[4,3,8,768]{3,2,1,0:T(8,128)(2,1)S(1)}, bf16[4,3,8,768]{3,2,1,0:T(8,128)(2,1)S(1)}, u32[]{:S(2)}, u32[]{:S(2)}) collective-permute-start(bf16[4,3,8,768]{3,2,1,0:T(8,128)(2,1)S(1)} %slice.479), channel_id=1, source_target_pairs={{0,2},{1,5},{2,0},{3,7},{4,6},{5,1},{6,4},{7,3},{8,10},{9,13},{10,... | collective-permute-start | bytes 442376 | tf_op jit(solution)/shard_map/ppermute | solution.py:482
  266.5 13.1 %collective-permute-start.13 = (bf16[8,9,8,768]{3,2,1,0:T(8,128)(2,1)S(1)}, bf16[8,9,8,768]{3,2,1,0:T(8,128)(2,1)S(1)}, u32[]{:S(2)}, u32[]{:S(2)}) collective-permute-start(bf16[8,9,8,768]{3,2,1,0:T(8,128)(2,1)S(1)} %add_convert_fusion.2), channel_id=1, source_target_pairs={{0,4},{1,3},{2,6},{3,1},{4,0},{5,7},{6,2},{7,5},{8,12},{9,11},{10,... | collective-permute-start | bytes 2654216 | tf_op jit(solution)/shard_map/ppermute | solution.py:482
  271.0 24.1 %collective-permute-start.23 = (bf16[8,12,8,768]{3,2,1,0:T(8,128)(2,1)S(1)}, bf16[8,12,8,768]{3,2,1,0:T(8,128)(2,1)S(1)}, u32[]{:S(2)}, u32[]{:S(2)}) collective-permute-start(bf16[8,12,8,768]{3,2,1,0:T(8,128)(2,1)S(1)} %copy-done.33), channel_id=1, source_target_pairs={{0,1},{1,0},{2,3},{3,2},{4,5},{5,4},{6,7},{7,6},{8,9},{9,8},{10,11... | collective-permute-start | bytes 3538952 | tf_op jit(solution)/shard_map/ppermute | solution.py:482
  271.1 27.6 %collective-permute-start.29 = (bf16[8,12,8,768]{3,2,1,0:T(8,128)(2,1)S(1)}, bf16[8,12,8,768]{3,2,1,0:T(8,128)(2,1)S(1)}, u32[]{:S(2)}, u32[]{:S(2)}) collective-permute-start(bf16[8,12,8,768]{3,2,1,0:T(8,128)(2,1)S(1)} %copy-done.32), channel_id=1, source_target_pairs={{0,1},{1,0},{2,3},{3,2},{4,5},{5,4},{6,7},{7,6},{8,9},{9,8},{10,11... | collective-permute-start | bytes 3538952 | tf_op jit(solution)/shard_map/ppermute | solution.py:482
  272.0 24.9 %collective-permute-start.25 = (bf16[8,12,8,768]{3,2,1,0:T(8,128)(2,1)S(1)}, bf16[8,12,8,768]{3,2,1,0:T(8,128)(2,1)S(1)}, u32[]{:S(2)}, u32[]{:S(2)}) collective-permute-start(bf16[8,12,8,768]{3,2,1,0:T(8,128)(2,1)S(1)} %add_convert_fusion.1), channel_id=1, source_target_pairs={{0,4},{1,3},{2,6},{3,1},{4,0},{5,7},{6,2},{7,5},{8,12},{9,11},{10,... | collective-permute-start | bytes 3538952 | tf_op jit(solution)/shard_map/ppermute | solution.py:482
  274.0 6.3 %copy-start.12 = (bf16[8,9,8,768]{3,2,1,0:T(8,128)(2,1)S(1)}, bf16[8,9,8,768]{3,2,1,0:T(8,128)(2,1)}, u32[]{:S(2)}) copy-start(bf16[8,9,8,768]{3,2,1,0:T(8,128)(2,1)} %get-tuple-element.96) | copy-start | bytes 2654212
  274.3 6.4 %collective-permute-start.21 = (bf16[2,3,8,768]{3,2,1,0:T(8,128)(2,1)S(1)}, bf16[2,3,8,768]{3,2,1,0:T(8,128)(2,1)S(1)}, u32[]{:S(2)}, u32[]{:S(2)}) collective-permute-start(bf16[2,3,8,768]{3,2,1,0:T(8,128)(2,1)S(1)} %slice.481), channel_id=1, source_target_pairs={{0,16},{1,9},{2,18},{3,11},{4,20},{5,13},{6,22},{7,15},{8,24},{9,1... | collective-permute-start | bytes 221192 | tf_op jit(solution)/shard_map/ppermute | solution.py:482
  279.6 36.3 %collective-permute-start.31 = (bf16[8,12,8,768]{3,2,1,0:T(8,128)(2,1)S(1)}, bf16[8,12,8,768]{3,2,1,0:T(8,128)(2,1)S(1)}, u32[]{:S(2)}, u32[]{:S(2)}) collective-permute-start(bf16[8,12,8,768]{3,2,1,0:T(8,128)(2,1)S(1)} %add_convert_fusion), channel_id=1, source_target_pairs={{0,4},{1,3},{2,6},{3,1},{4,0},{5,7},{6,2},{7,5},{8,12},{9,11},{10,... | collective-permute-start | bytes 3538952 | tf_op jit(solution)/shard_map/ppermute | solution.py:482
  280.7 13.2 %collective-permute-start.14 = (bf16[4,9,8,768]{3,2,1,0:T(8,128)(2,1)S(1)}, bf16[4,9,8,768]{3,2,1,0:T(8,128)(2,1)S(1)}, u32[]{:S(2)}, u32[]{:S(2)}) collective-permute-start(bf16[4,9,8,768]{3,2,1,0:T(8,128)(2,1)S(1)} %slice.473), channel_id=1, source_target_pairs={{0,2},{1,5},{2,0},{3,7},{4,6},{5,1},{6,4},{7,3},{8,10},{9,13},{10,... | collective-permute-start | bytes 1327112 | tf_op jit(solution)/shard_map/ppermute | solution.py:482
  282.7 14.2 %copy-start.8 = (bf16[8,12,8,768]{3,2,1,0:T(8,128)(2,1)S(1)}, bf16[8,12,8,768]{3,2,1,0:T(8,128)(2,1)}, u32[]{:S(2)}) copy-start(bf16[8,12,8,768]{3,2,1,0:T(8,128)(2,1)} %get-tuple-element.105) | copy-start | bytes 3538948
  293.9 23.4 %collective-permute-start.22 = (bf16[1,3,8,768]{3,2,1,0:T(8,128)(2,1)S(1)}, bf16[1,3,8,768]{3,2,1,0:T(8,128)(2,1)S(1)}, u32[]{:S(2)}, u32[]{:S(2)}) collective-permute-start(bf16[1,3,8,768]{3,2,1,0:T(8,128)(2,1)S(1)} %slice.482), channel_id=1, source_target_pairs={{0,8},{1,17},{2,10},{3,19},{4,12},{5,21},{6,14},{7,23},{8,0},{9,25... | collective-permute-start | bytes 110600 | tf_op jit(solution)/shard_map/ppermute | solution.py:482
  295.2 22.7 %collective-permute-start.15 = (bf16[2,9,8,768]{3,2,1,0:T(8,128)(2,1)S(1)}, bf16[2,9,8,768]{3,2,1,0:T(8,128)(2,1)S(1)}, u32[]{:S(2)}, u32[]{:S(2)}) collective-permute-start(bf16[2,9,8,768]{3,2,1,0:T(8,128)(2,1)S(1)} %slice.476), channel_id=1, source_target_pairs={{0,16},{1,9},{2,18},{3,11},{4,20},{5,13},{6,22},{7,15},{8,24},{9,1... | collective-permute-start | bytes 663560 | tf_op jit(solution)/shard_map/ppermute | solution.py:482
  297.3 18.6 %copy-start.7 = (bf16[8,12,8,768]{3,2,1,0:T(8,128)(2,1)S(1)}, bf16[8,12,8,768]{3,2,1,0:T(8,128)(2,1)}, u32[]{:S(2)}) copy-start(bf16[8,12,8,768]{3,2,1,0:T(8,128)(2,1)} %get-tuple-element.109) | copy-start | bytes 3538948
  297.4 21.7 %collective-permute-start.26 = (bf16[4,12,8,768]{3,2,1,0:T(8,128)(2,1)S(1)}, bf16[4,12,8,768]{3,2,1,0:T(8,128)(2,1)S(1)}, u32[]{:S(2)}, u32[]{:S(2)}) collective-permute-start(bf16[4,12,8,768]{3,2,1,0:T(8,128)(2,1)S(1)} %slice.472), channel_id=1, source_target_pairs={{0,2},{1,5},{2,0},{3,7},{4,6},{5,1},{6,4},{7,3},{8,10},{9,13},{10,... | collective-permute-start | bytes 1769480 | tf_op jit(solution)/shard_map/ppermute | solution.py:482
  316.4 9.9 %collective-permute-start.32 = (bf16[4,12,8,768]{3,2,1,0:T(8,128)(2,1)S(1)}, bf16[4,12,8,768]{3,2,1,0:T(8,128)(2,1)S(1)}, u32[]{:S(2)}, u32[]{:S(2)}) collective-permute-start(bf16[4,12,8,768]{3,2,1,0:T(8,128)(2,1)S(1)} %slice.471), channel_id=1, source_target_pairs={{0,2},{1,5},{2,0},{3,7},{4,6},{5,1},{6,4},{7,3},{8,10},{9,13},{10,... | collective-permute-start | bytes 1769480 | tf_op jit(solution)/shard_map/ppermute | solution.py:482
  318.0 10.3 %collective-permute-start.16 = (bf16[1,9,8,768]{3,2,1,0:T(8,128)(2,1)S(1)}, bf16[1,9,8,768]{3,2,1,0:T(8,128)(2,1)S(1)}, u32[]{:S(2)}, u32[]{:S(2)}) collective-permute-start(bf16[1,9,8,768]{3,2,1,0:T(8,128)(2,1)S(1)} %slice.480), channel_id=1, source_target_pairs={{0,8},{1,17},{2,10},{3,19},{4,12},{5,21},{6,14},{7,23},{8,0},{9,25... | collective-permute-start | bytes 331784 | tf_op jit(solution)/shard_map/ppermute | solution.py:482
  319.3 10.4 %collective-permute-start.27 = (bf16[2,12,8,768]{3,2,1,0:T(8,128)(2,1)S(1)}, bf16[2,12,8,768]{3,2,1,0:T(8,128)(2,1)S(1)}, u32[]{:S(2)}, u32[]{:S(2)}) collective-permute-start(bf16[2,12,8,768]{3,2,1,0:T(8,128)(2,1)S(1)} %slice.475), channel_id=1, source_target_pairs={{0,16},{1,9},{2,18},{3,11},{4,20},{5,13},{6,22},{7,15},{8,24},{9,1... | collective-permute-start | bytes 884744 | tf_op jit(solution)/shard_map/ppermute | solution.py:482
  326.5 14.0 %collective-permute-start.33 = (bf16[2,12,8,768]{3,2,1,0:T(8,128)(2,1)S(1)}, bf16[2,12,8,768]{3,2,1,0:T(8,128)(2,1)S(1)}, u32[]{:S(2)}, u32[]{:S(2)}) collective-permute-start(bf16[2,12,8,768]{3,2,1,0:T(8,128)(2,1)S(1)} %slice.474), channel_id=1, source_target_pairs={{0,16},{1,9},{2,18},{3,11},{4,20},{5,13},{6,22},{7,15},{8,24},{9,1... | collective-permute-start | bytes 884744 | tf_op jit(solution)/shard_map/ppermute | solution.py:482
  329.7 10.9 %collective-permute-start.28 = (bf16[1,12,8,768]{3,2,1,0:T(8,128)(2,1)S(1)}, bf16[1,12,8,768]{3,2,1,0:T(8,128)(2,1)S(1)}, u32[]{:S(2)}, u32[]{:S(2)}) collective-permute-start(bf16[1,12,8,768]{3,2,1,0:T(8,128)(2,1)S(1)} %slice.478), channel_id=1, source_target_pairs={{0,8},{1,17},{2,10},{3,19},{4,12},{5,21},{6,14},{7,23},{8,0},{9,25... | collective-permute-start | bytes 442376 | tf_op jit(solution)/shard_map/ppermute | solution.py:482
  340.5 5.2 %collective-permute-start.34 = (bf16[1,12,8,768]{3,2,1,0:T(8,128)(2,1)S(1)}, bf16[1,12,8,768]{3,2,1,0:T(8,128)(2,1)S(1)}, u32[]{:S(2)}, u32[]{:S(2)}) collective-permute-start(bf16[1,12,8,768]{3,2,1,0:T(8,128)(2,1)S(1)} %slice.477), channel_id=1, source_target_pairs={{0,8},{1,17},{2,10},{3,19},{4,12},{5,21},{6,14},{7,23},{8,0},{9,25... | collective-permute-start | bytes 442376 | tf_op jit(solution)/shard_map/ppermute | solution.py:482
  (25 other events, 55.4 us)
Sparse Core Ops, SparseCore 0:
  10.9 98.7 all-gather.1
